TPU v7x, 1024 devices: a whole 8x8x8 slice. The times are simulated.
1024 devices in a mesh: gx: 64 (over x, z), gy: 16 (over y, core).
Axes of the slice: x: 8, y: 8, z: 8, core: 2. Of those that a mesh axis runs over, the one named last changes fastest.
Arguments:
- state: float32 [5, 192, 256, 128], P(None, 'gx', 'gy'), may hold values from -2 to 6, as said below
- lf_speed: float32 [3], replicated, may hold values from 2.5 to 4
- ghost_cell: int32 [64, 16, 16, 192], P('gx', 'gy'), may hold values from -1 to 6143, as said below
- ghost_frac: float32 [3, 64, 16, 16, 192], P(None, 'gx', 'gy'), may hold values from 0 to 1
- donor_block: int32 [64, 16, 16, 192], P('gx', 'gy'), may hold values from 0 to 3966, as said below
Outputs:
- advanced: float32 [5, 192, 256, 128], P(None, 'gx', 'gy')
Inputs may be any that keep to these rules, and one draw needn't show every extreme that they name: `state`: state of an ideal gas with ratio of specific heats 1.4: density and pressure lie between 0.49 and 2.02 in every cell. `ghost_cell`: -1 marks an empty slot, and in each list [x, p, q, :] the live slots come first. A live slot holds (i * 16 + j) * 128 + k for a cell of brick (x, p); no cell appears twice among the lists of a brick. In every draw each x column has a brick whose lists are full from every q. `donor_block`: holds (i * 16 + j) * 128 + k for a cell of brick (x, q) with i <= 1, j <= 14, k <= 126; entry [x, q, p, s] serves slot s of ghost_cell[x, p, q]; entries of empty slots are arbitrary within the range.
All inputs are finite; a program needn't handle non-finite values.
Results may differ from a plain program's by a relative error of at most 0.0003.
Values sent between devices are 32-bit elements; how exact they have to be, the bound alone decides.
A program may use at most 32 MiB of HBM per device.

v0:
```python
import jax
import jax.numpy as jnp
from jax import lax
from jax.sharding import PartitionSpec as P

heat_ratio = 1.4
time_step = 0.25
small_eps = 1e-06
wall_sign = (1.0, -1.0, -1.0, -1.0, 1.0)


def extended(block, sides, width):
    for axis, dim in sides:
        count = lax.axis_size(axis)
        forward = [(i, i + 1) for i in range(count - 1)]
        backward = [(target, source) for source, target in forward]
        low = lax.ppermute(
            lax.slice_in_dim(block, block.shape[dim] - width, None, axis=dim), axis, forward
        )
        high = lax.ppermute(lax.slice_in_dim(block, 0, width, axis=dim), axis, backward)
        block = jnp.concatenate([low, block, high], axis=dim)
    return block


def smoothed(far_left, near_left, center, near_right, far_right):
    beta_zero = (
        13.0 / 12.0 * (far_left - 2.0 * near_left + center) ** 2
        + 0.25 * (far_left - 4.0 * near_left + 3.0 * center) ** 2
    )
    beta_one = (
        13.0 / 12.0 * (near_left - 2.0 * center + near_right) ** 2
        + 0.25 * (near_left - near_right) ** 2
    )
    beta_two = (
        13.0 / 12.0 * (center - 2.0 * near_right + far_right) ** 2
        + 0.25 * (3.0 * center - 4.0 * near_right + far_right) ** 2
    )
    weight_zero = 0.1 / (small_eps + beta_zero) ** 2
    weight_one = 0.6 / (small_eps + beta_one) ** 2
    weight_two = 0.3 / (small_eps + beta_two) ** 2
    guess_zero = (2.0 * far_left - 7.0 * near_left + 11.0 * center) / 6.0
    guess_one = (-near_left + 5.0 * center + 2.0 * near_right) / 6.0
    guess_two = (2.0 * center + 5.0 * near_right - far_right) / 6.0
    return (weight_zero * guess_zero + weight_one * guess_one + weight_two * guess_two) / (
        weight_zero + weight_one + weight_two
    )


def primitive(conserved):
    density = conserved[0]
    velocity = conserved[1:4] / density[None]
    pressure = (heat_ratio - 1.0) * (
        conserved[4] - 0.5 * jnp.sum(conserved[1:4] * velocity, axis=0)
    )
    return jnp.concatenate([density[None], velocity, pressure[None]], axis=0)


def flux_change(prim_field, sweep_axis, lf_value, direction):
    density = prim_field[0]
    velocity = prim_field[1:4]
    pressure = prim_field[4]
    normal = velocity[direction]
    energy = pressure / (heat_ratio - 1.0) + 0.5 * density * jnp.sum(velocity * velocity, axis=0)
    momenta = density[None] * velocity
    conserved = jnp.concatenate([density[None], momenta, energy[None]], axis=0)
    momentum_flux = momenta * normal[None]
    momentum_flux = momentum_flux.at[direction].add(pressure)
    fluxes = jnp.concatenate(
        [(density * normal)[None], momentum_flux, (normal * (energy + pressure))[None]], axis=0
    )
    upwind = 0.5 * (fluxes + lf_value * conserved)
    downwind = 0.5 * (fluxes - lf_value * conserved)
    interior = prim_field.shape[sweep_axis] - 6

    def window(values, offset):
        return lax.slice_in_dim(values, offset, offset + interior + 1, axis=sweep_axis)

    face_flux = smoothed(
        window(upwind, 0),
        window(upwind, 1),
        window(upwind, 2),
        window(upwind, 3),
        window(upwind, 4),
    )
    face_flux = face_flux + smoothed(
        window(downwind, 5),
        window(downwind, 4),
        window(downwind, 3),
        window(downwind, 2),
        window(downwind, 1),
    )
    return lax.slice_in_dim(face_flux, 1, interior + 1, axis=sweep_axis) - lax.slice_in_dim(
        face_flux, 0, interior, axis=sweep_axis
    )


def corner_weights(fractions):
    result = []
    for corner in range(8):
        part_x = fractions[0] if corner // 4 == 1 else 1.0 - fractions[0]
        part_y = fractions[1] if corner // 2 % 2 == 1 else 1.0 - fractions[1]
        part_z = fractions[2] if corner % 2 == 1 else 1.0 - fractions[2]
        result.append(part_x * part_y * part_z)
    return result


def edge_fill(values, sweep_axis, position, extent):
    length = values.shape[sweep_axis]
    low_edge = lax.slice_in_dim(values, 3, 4, axis=sweep_axis)
    high_edge = lax.slice_in_dim(values, length - 4, length - 3, axis=sweep_axis)
    shape_one = [1] * values.ndim
    shape_one[sweep_axis] = length
    index_row = lax.broadcasted_iota(jnp.int32, (length,), 0).reshape(shape_one)
    values = jnp.where((index_row < 3) & (position == 0), low_edge, values)
    values = jnp.where((index_row >= length - 3) & (position == extent - 1), high_edge, values)
    return values


def on_device(state, lf_speed, ghost_cell, ghost_frac, donor_block):
    size_x, size_y, size_z = (state.shape[1], state.shape[2], state.shape[3])
    cell_count = size_x * size_y * size_z
    flat_state = state.reshape(5, cell_count)
    donor_base = donor_block[0, 0]
    ghost_list = ghost_cell[0, 0]
    own_fracs = ghost_frac[:, 0, 0]
    offsets = [
        corner // 4 * size_y * size_z + corner // 2 % 2 * size_z + corner % 2 for corner in range(8)
    ]
    donors = jnp.stack([flat_state[:, donor_base + offset] for offset in offsets], axis=1)
    arrived = lax.all_to_all(donors, "gy", split_axis=2, concat_axis=2, tiled=True)
    weights = corner_weights(own_fracs)
    image_value = jnp.zeros((5,) + donor_base.shape, jnp.float32)
    for corner in range(8):
        image_value = image_value + weights[corner][None] * arrived[:, corner]
    wall_signs = jnp.array(wall_sign, jnp.float32)[:, None, None]
    ghost_values = (image_value * wall_signs).reshape(5, -1)
    target = jnp.where(ghost_list >= 0, ghost_list, cell_count).reshape(-1)
    filled = flat_state.at[:, target].set(ghost_values, mode="drop").reshape(state.shape)
    frozen = (
        jnp.zeros((cell_count,), jnp.int32).at[target].set(1, mode="drop").reshape(state.shape[1:])
    )
    prim_field = primitive(filled)
    padded = extended(prim_field, (("gx", 1), ("gy", 2)), 3)
    padded = edge_fill(padded, 1, lax.axis_index("gx"), lax.axis_size("gx"))
    padded = edge_fill(padded, 2, lax.axis_index("gy"), lax.axis_size("gy"))
    change = flux_change(padded[:, :, 3:-3, :], 1, lf_speed[0], 0)
    change = change + flux_change(padded[:, 3:-3, :, :], 2, lf_speed[1], 1)
    z_padded = jnp.pad(prim_field, ((0, 0), (0, 0), (0, 0), (3, 3)), mode="edge")
    change = change + flux_change(z_padded, 3, lf_speed[2], 2)
    return jnp.where(frozen[None] == 1, filled, filled - time_step * change)


def solution(mesh):
    in_specs = (
        P(None, "gx", "gy", None),
        P(),
        P("gx", "gy", None, None),
        P(None, "gx", "gy", None, None),
        P("gx", "gy", None, None),
    )
    out_specs = P(None, "gx", "gy", None)
    return jax.shard_map(
        on_device, mesh=mesh, in_specs=in_specs, out_specs=out_specs, check_vma=False
    )
```

profile of v0, /device:TPU:15, one launch (start us, length us, event | category | flops | bytes accessed | tf_op | source)
XLA Modules:
  0.0 235.3 jit_solution(5074192429747870122)
XLA Ops:
  3.3 10.9 %gather_fusion = f32[3072,5]{1,0:T(8,128)} fusion(f32[5,6144]{0,1:T(8,128)S(1)} %bitcast.191, s32[3072]{0:T(1024)S(1)} %get-tuple-element.126), kind=kCustom, calls=%fused_computation | custom fusion | bytes 135168 | tf_op jit(solution)/shard_map/gather | solution.py:129
  14.2 2.0 copy.72
  16.9 10.9 %gather_fusion.1 = f32[3072,5]{1,0:T(8,128)} fusion(f32[5,6144]{0,1:T(8,128)S(1)} %bitcast.192, s32[3072]{0:T(1024)S(1)} %get-tuple-element.125), kind=kCustom, calls=%fused_computation.1 | custom fusion | bytes 135168 | tf_op jit(solution)/shard_map/gather | solution.py:129
  27.8 2.0 copy.73
  30.0 10.9 %gather_fusion.2 = f32[3072,5]{1,0:T(8,128)} fusion(f32[5,6144]{0,1:T(8,128)S(1)} %bitcast.193, s32[3072]{0:T(1024)S(1)} %get-tuple-element.124), kind=kCustom, calls=%fused_computation.2 | custom fusion | bytes 135168 | tf_op jit(solution)/shard_map/gather | solution.py:129
  42.9 10.9 %gather_fusion.3 = f32[3072,5]{1,0:T(8,128)} fusion(f32[5,6144]{0,1:T(8,128)S(1)} %bitcast.194, s32[3072]{0:T(1024)S(1)} %get-tuple-element.123), kind=kCustom, calls=%fused_computation.3 | custom fusion | bytes 135168 | tf_op jit(solution)/shard_map/gather | solution.py:129
  56.0 10.9 %gather_fusion.4 = f32[3072,5]{1,0:T(8,128)} fusion(f32[5,6144]{0,1:T(8,128)S(1)} %bitcast.195, s32[3072]{0:T(1024)S(1)} %get-tuple-element.122), kind=kCustom, calls=%fused_computation.4 | custom fusion | bytes 135168 | tf_op jit(solution)/shard_map/gather | solution.py:129
  68.9 10.9 %gather_fusion.5 = f32[3072,5]{1,0:T(8,128)} fusion(f32[5,6144]{0,1:T(8,128)S(1)} %bitcast.196, s32[3072]{0:T(1024)S(1)} %get-tuple-element.121), kind=kCustom, calls=%fused_computation.5 | custom fusion | bytes 135168 | tf_op jit(solution)/shard_map/gather | solution.py:129
  86.0 11.9 %gather_fusion.6 = f32[3072,5]{1,0:T(8,128)} fusion(f32[5,6144]{0,1:T(8,128)S(1)} %bitcast.197, s32[3072]{0:T(1024)} %get-tuple-element.120), kind=kCustom, calls=%fused_computation.6 | custom fusion | bytes 135168 | tf_op jit(solution)/shard_map/gather | solution.py:129
  97.9 2.7 %copy.78 = f32[16,192,5]{1,0,2:T(8,128)} copy(f32[16,192,5]{2,1,0:T(8,128)} %bitcast.216) | data formatting | bytes 122880 | tf_op jit(solution)/shard_map/gather | solution.py:129
  100.5 11.9 %gather_fusion.7 = f32[3072,5]{1,0:T(8,128)} fusion(f32[5,6144]{0,1:T(8,128)S(1)} %bitcast.198, s32[3072]{0:T(1024)} %get-tuple-element.119), kind=kCustom, calls=%fused_computation.7 | custom fusion | bytes 135168 | tf_op jit(solution)/shard_map/gather | solution.py:129
  112.4 2.7 %copy.79 = f32[16,192,5]{1,0,2:T(8,128)} copy(f32[16,192,5]{2,1,0:T(8,128)} %bitcast.217) | data formatting | bytes 122880 | tf_op jit(solution)/shard_map/gather | solution.py:129
  121.4 2.3 copy.80
  123.7 8.2 %all-to-all-start = ((f32[5,8,16,192]{3,1,0,2:T(8,128)}), f32[5,8,16,192]{3,1,0,2:T(8,128)}, u32[]{:S(2)}, u32[]{:S(2)}) async-start(f32[5,8,16,192]{3,1,0,2:T(8,128)} %copy.80), calls=%async_computation | async-start | bytes 1310720 | tf_op jit(solution)/shard_map/all_to_all | solution.py:130
  132.3 11.8 %scatter_custom_fusion = s32[6144]{0:T(1024)S(1)} fusion(s32[3072]{0:T(1024)S(1)} %bitcast.224, s32[3072]{0:T(1024)S(1)} %broadcast.597, s32[]{:T(128)} %constant.191.clone.1), kind=kCustom, calls=%fused_computation.120 | custom fusion | bytes 24580 | tf_op jit(solution)/shard_map/scatter | solution.py:140
  147.2 4.9 %all-to-all-done = f32[5,8,16,192]{3,1,0,2:T(8,128)} async-done(((f32[5,8,16,192]{3,1,0,2:T(8,128)}), f32[5,8,16,192]{3,1,0,2:T(8,128)}, u32[]{:S(2)}, u32[]{:S(2)}) %all-to-all-start) | async-done | bytes 491552 | tf_op jit(solution)/shard_map/all_to_all | solution.py:130
  152.1 4.5 %fusion.20 = (f32[5,1,16,192]{3,1,0,2:T(1,128)S(1)}, f32[5,1,16,192]{3,1,0,2:T(1,128)S(1)}, f32[5,1,16,192]{3,1,0,2:T(1,128)}, f32[5,1,16,192]{3,1,0,2:T(1,128)}...) fusion(f32[5,8,16,192]{3,1,0,2:T(8,128)} %all-to-all-done), kind=kLoop, calls=%fused_computation.149 | loop fusion | bytes 983040 | tf_op jit(solution)/shard_map/slice | solution.py:134
  179.2 9.8 %scatter_fusion = f32[5,6144]{0,1:T(8,128)S(1)} fusion(f32[5,6144]{0,1:T(8,128)S(1)} %bitcast.199, s32[3072]{0:T(1024)} %bitcast.225, f32[3072,5]{1,0:T(8,128)} %copy.89), kind=kCustom, calls=%fused_computation.9 | custom fusion | bytes 196608 | tf_op jit(solution)/shard_map/scatter | solution.py:138
  188.9 2.5 %slice_reduce_fusion.1 = (f32[6144]{0:T(1024)S(1)}, f32[6144]{0:T(1024)S(1)}) fusion(f32[5,6144]{0,1:T(8,128)S(1)} %scatter_fusion), kind=kLoop, calls=%fused_computation.12 | loop fusion | bytes 98304 | tf_op jit(solution)/shard_map/slice | solution.py:50
  191.5 3.7 %fusion.19 = (f32[3,6144]{0,1:T(8,128)}, f32[6144]{0:T(1024)S(1)}) fusion(f32[5,6144]{0,1:T(8,128)S(1)} %scatter_fusion, f32[6144]{0:T(1024)S(1)} %get-tuple-element.41), kind=kLoop, calls=%fused_computation.148 | loop fusion | flops 49152 | bytes 196608 | tf_op jit(solution)/shard_map/slice | solution.py:51
  195.1 2.4 %copy.97 = f32[3,3,16,128]{3,2,1,0:T(8,128)S(1)} copy(f32[3,3,16,128]{0,3,2,1:T(8,128)} %bitcast.201) | data formatting | bytes 147456 | tf_op jit(solution)/shard_map/slice | solution.py:51
  197.5 4.9 %collective-permute-start = (f32[5,3,16,128]{3,2,1,0:T(8,128)S(1)}, f32[5,3,16,128]{3,2,1,0:T(8,128)S(1)}, u32[]{:S(2)}, u32[]{:S(2)}) collective-permute-start(f32[5,3,16,128]{3,2,1,0:T(8,128)S(1)} %pad_maximum_fusion.5), channel_id=1, source_target_pairs={{0,16},{16,32},{32,48},{48,64},{64,80},{80,96},{96,112},{112,128},... | collective-permute-start | bytes 368648 | tf_op jit(solution)/shard_map/ppermute | solution.py:17
  202.5 14.9 %collective-permute-start.1 = (f32[5,3,16,128]{3,2,1,0:T(8,128)S(1)}, f32[5,3,16,128]{3,2,1,0:T(8,128)S(1)}, u32[]{:S(2)}, u32[]{:S(2)}) collective-permute-start(f32[5,3,16,128]{3,2,1,0:T(8,128)S(1)} %pad_maximum_fusion.5), channel_id=1, source_target_pairs={{16,0},{32,16},{48,32},{64,48},{80,64},{96,80},{112,96},{128,112},... | collective-permute-start | bytes 368648 | tf_op jit(solution)/shard_map/ppermute | solution.py:20
  222.0 3.0 %collective-permute-start.3 = (f32[5,9,3,128]{3,2,1,0:T(4,128)}, f32[5,9,3,128]{3,2,1,0:T(4,128)}, u32[]{:S(2)}, u32[]{:S(2)}) collective-permute-start(f32[5,9,3,128]{3,2,1,0:T(4,128)} %get-tuple-element.95), channel_id=1, source_target_pairs={{1,0},{2,1},{3,2},{4,3},{5,4},{6,5},{7,6},{8,7},{9,8},{10,9},{11,1... | collective-permute-start | bytes 207368 | tf_op jit(solution)/shard_map/ppermute | solution.py:20
  (117 shorter events, 63.4 us)
Async XLA Ops:
  117.6 14.3 %copy-start.5 = (s32[1,1,16,192]{3,2,1,0:T(8,128)S(1)}, s32[1,1,16,192]{3,2,1,0:T(8,128)}, u32[]{:S(2)}) copy-start(s32[1,1,16,192]{3,2,1,0:T(8,128)} %param.14) | copy-start | bytes 36868
  117.6 14.4 %copy-start.3 = (f32[3,1,1,16,192]{4,3,2,1,0:T(8,128)S(1)}, f32[3,1,1,16,192]{4,3,2,1,0:T(8,128)}, u32[]{:S(2)}) copy-start(f32[3,1,1,16,192]{4,3,2,1,0:T(8,128)} %param.15) | copy-start | bytes 110596
  119.8 25.5 %copy-start.6 = (f32[3]{0:T(128)S(1)}, f32[3]{0:T(128)}, u32[]{:S(2)}) copy-start(f32[3]{0:T(128)} %param.13) | copy-start | bytes 40
  123.7 28.4 %all-to-all-start = ((f32[5,8,16,192]{3,1,0,2:T(8,128)}), f32[5,8,16,192]{3,1,0,2:T(8,128)}, u32[]{:S(2)}, u32[]{:S(2)}) async-start(f32[5,8,16,192]{3,1,0,2:T(8,128)} %copy.80), calls=%async_computation | async-start | bytes 1310720 | tf_op jit(solution)/shard_map/all_to_all | solution.py:130
  132.1 15.1 %copy-start.2 = (s32[3072,1]{0,1:T(1,128)}, s32[3072,1]{0,1:T(1,128)S(1)}, u32[]{:S(2)}) copy-start(s32[3072,1]{0,1:T(1,128)S(1)} %compare_select_fusion) | copy-start | bytes 36868
  197.5 21.4 %collective-permute-start = (f32[5,3,16,128]{3,2,1,0:T(8,128)S(1)}, f32[5,3,16,128]{3,2,1,0:T(8,128)S(1)}, u32[]{:S(2)}, u32[]{:S(2)}) collective-permute-start(f32[5,3,16,128]{3,2,1,0:T(8,128)S(1)} %pad_maximum_fusion.5), channel_id=1, source_target_pairs={{0,16},{16,32},{32,48},{48,64},{64,80},{80,96},{96,112},{112,128},... | collective-permute-start | bytes 368648 | tf_op jit(solution)/shard_map/ppermute | solution.py:17
  202.5 16.9 %collective-permute-start.1 = (f32[5,3,16,128]{3,2,1,0:T(8,128)S(1)}, f32[5,3,16,128]{3,2,1,0:T(8,128)S(1)}, u32[]{:S(2)}, u32[]{:S(2)}) collective-permute-start(f32[5,3,16,128]{3,2,1,0:T(8,128)S(1)} %pad_maximum_fusion.5), channel_id=1, source_target_pairs={{16,0},{32,16},{48,32},{64,48},{80,64},{96,80},{112,96},{128,112},... | collective-permute-start | bytes 368648 | tf_op jit(solution)/shard_map/ppermute | solution.py:20
  220.1 8.7 %collective-permute-start.2 = (f32[5,9,3,128]{3,2,1,0:T(4,128)}, f32[5,9,3,128]{3,2,1,0:T(4,128)}, u32[]{:S(2)}, u32[]{:S(2)}) collective-permute-start(f32[5,9,3,128]{3,2,1,0:T(4,128)} %get-tuple-element.94), channel_id=1, source_target_pairs={{0,1},{1,2},{2,3},{3,4},{4,5},{5,6},{6,7},{7,8},{8,9},{9,10},{10,1... | collective-permute-start | bytes 207368 | tf_op jit(solution)/shard_map/ppermute | solution.py:17
  222.0 6.8 %collective-permute-start.3 = (f32[5,9,3,128]{3,2,1,0:T(4,128)}, f32[5,9,3,128]{3,2,1,0:T(4,128)}, u32[]{:S(2)}, u32[]{:S(2)}) collective-permute-start(f32[5,9,3,128]{3,2,1,0:T(4,128)} %get-tuple-element.95), channel_id=1, source_target_pairs={{1,0},{2,1},{3,2},{4,3},{5,4},{6,5},{7,6},{8,7},{9,8},{10,9},{11,1... | collective-permute-start | bytes 207368 | tf_op jit(solution)/shard_map/ppermute | solution.py:20
  226.9 2.9 %copy-start.8 = (pred[9]{0:T(512)(128)(4,1)S(1)}, pred[9]{0:T(512)(128)(4,1)}, u32[]{:S(2)}) copy-start(pred[9]{0:T(512)(128)(4,1)} %get-tuple-element.127) | copy-start | bytes 31
  226.9 2.9 %copy-start.9 = (pred[9]{0:T(512)(128)(4,1)S(1)}, pred[9]{0:T(512)(128)(4,1)}, u32[]{:S(2)}) copy-start(pred[9]{0:T(512)(128)(4,1)} %get-tuple-element.128) | copy-start | bytes 31
  228.7 2.3 copy-start.7
  232.9 1.6 copy-start
  232.9 1.6 copy-start.1
  232.9 1.6 copy-start.4
where the time goes:
time: 237 us; the launch traced here: 235 us
  local copies, waits for them, and re-layouts  176 us (74%)
  starting transfers between devices  33 us (14%)
  other arithmetic  20.1 us (8%)
  waiting for transfers between devices  5.34 us (2%)
    gather x16, local copies, waits for them, and re-layouts, on_device(): flat_state[:, donor_base + offset]  107 us
    ppermute x2, starting transfers between devices, extended(): lax.ppermute(lax.slice_in_dim(block, 0, width, axis=dim), axis, backward)  17.9 us
    slice x9, local copies, waits for them, and re-layouts, on_device(): image_value = image_value + weights[corner][None] * arrived[:, corner]  13.1 us
    scatter x1, local copies, waits for them, and re-layouts, on_device(): jnp.zeros((cell_count,), jnp.int32).at[target].set(1, mode='drop')  11.8 us
    squeeze x8, local copies, waits for them, and re-layouts, on_device(): image_value = image_value + weights[corner][None] * arrived[:, corner]  11 us
    scatter x1, local copies, waits for them, and re-layouts, on_device(): flat_state.at[:, target].set(ghost_values, mode='drop').reshape(state.shape)  9.76 us
    all_to_all x1, starting transfers between devices, on_device(): lax.all_to_all(donors, 'gy', split_axis=2, concat_axis=2, tiled=True)  8.24 us
    unnamed x28, local copies, waits for them, and re-layouts  7.23 us
  transfers between devices with their start and end apart: 5, of which 2 were waited for; matrix products, arithmetic and copies ran while one was open for 9% of the time, Pallas kernels for 0%

commit v1 on v0

v1 whole, which is shorter than its diff:
```python
import functools

import jax
import jax.numpy as jnp
from jax import lax
from jax.experimental import pallas as pl
from jax.experimental.pallas import tpu as pltpu
from jax.sharding import PartitionSpec as P

MESH = pl.DeviceIdType.MESH
F32 = jnp.float32
BF16 = jnp.bfloat16
SIGN = (1.0, -1.0, -1.0, -1.0, 1.0)
EPS = 16.0e-6
C13 = 13.0 / 3.0
NX, NY, NZ = 3, 16, 128
ROWS = 24


def loop(count, body):
    def step(i, carry):
        body(i)
        return carry

    lax.fori_loop(0, count, step, 0, unroll=True)


def sq(x):
    return x * x


def rcp(x):
    r = pl.reciprocal(x, approx=True)
    return r * (2.0 - x * r)


def iota(shape, dim):
    return lax.broadcasted_iota(jnp.int32, shape, dim)


def betas(w):
    n = w.shape[0] - 4
    d = w[1:] - w[:-1]
    dd = d[1:] - d[:-1]
    e = (C13 * dd) * dd + EPS
    t = dd[1:] - dd[:-1]
    left = e[:n] + sq(3.0 * d[1 : n + 1] - d[:n])
    mid = e[1 : n + 1] + sq(d[1 : n + 1] + d[2 : n + 2])
    right = e[2 : n + 2] + sq(3.0 * d[2 : n + 2] - d[3 : n + 3])
    return w[2 : n + 2], d[1 : n + 1], d[2 : n + 2], t[:n], t[1:], left, mid, right


def upwind(f, dm, dp, tm, tp, left, mid, right):
    a, b, c = sq(mid * right), sq(left * right), 3.0 * sq(left * mid)
    return 6.0 * f + dm + 2.0 * dp - (2.0 * a * tm + c * tp) * rcp(a + 6.0 * b + c)


def downwind(f, dm, dp, tm, tp, left, mid, right):
    a, b, c = sq(mid * left), sq(left * right), 3.0 * sq(mid * right)
    return 6.0 * f - dp - 2.0 * dm + (2.0 * a * tp + c * tm) * rcp(a + 6.0 * b + c)


def z_change(fp, fm):
    lane = iota(fp.shape, 1)
    first, last = lane == 0, lane == NZ - 1
    down = lambda x: pltpu.roll(x, 1, 1)
    up = lambda x: pltpu.roll(x, NZ - 1, 1)

    def parts(f):
        dp = jnp.where(last, 0.0, up(f) - f)
        dm = down(dp)
        dd = dp - dm
        e = (C13 * dd) * dd + EPS
        left, right = e + sq(3.0 * dp - dm), e + sq(3.0 * dm - dp)
        mid = e + sq(dp + dm)
        tm = dd - jnp.where(first, 0.0, down(dd))
        tp = jnp.where(last, 0.0, up(dd)) - dd
        args = (f, dm, dp, tm, tp, jnp.where(first, EPS, down(left)), mid, jnp.where(last, EPS, up(right)))
        return args, dd, left, right

    plus, dd_plus, _, right = parts(fp)
    minus, dd_minus, left, _ = parts(fm)
    rp, rm = upwind(*plus), downwind(*minus)
    f = jnp.where(first, fp, fm)
    dd = jnp.where(first, dd_plus, dd_minus)
    far = jnp.where(first, right, left)
    edge = 6.0 * f - 3.0 * EPS * EPS * dd * rcp(7.0 * sq(far) + 3.0 * EPS * EPS)
    return rp - jnp.where(first, edge, down(rp)) + jnp.where(last, edge, up(rm)) - rm


def inverse_pressure(u):
    rinv = 1.0 / u[0]
    kinetic = (u[1] * u[1] + u[2] * u[2] + u[3] * u[3]) * rinv
    return rinv, 0.4 * (u[4] - 0.5 * kinetic)


def split(u, rinv, p, direction, speed):
    normal = u[1 + direction] * rinv
    result = []
    for v in range(5):
        if v == 0:
            f = u[1 + direction]
        elif v == 4:
            f = normal * (u[4] + p)
        else:
            f = normal * u[v]
            if v == 1 + direction:
                f = f + p
        s = speed * u[v]
        result.append((f + s, f - s))
    return result


def kernel(
    n_gx, n_gy, lf, state_h, cell_h, frac_h, donor_h, out_h,
    stv, cellv, fracv, donv, fsend, frecv, isend, irecv, kq, cq, fq, ss, pp, bs, ohs, am, maskv,
    fil, xl, xr, yl, yr, fx, fy, fz, fluxy, chg, outv,
    in_sem, fs_sem, fr_sem, is_sem, ir_sem, hs_sem, hr_sem, out_sem,
):
    gx, gy = lax.axis_index("gx"), lax.axis_index("gy")
    right, left = lax.rem(gx + 1, n_gx), lax.rem(gx + n_gx - 1, n_gx)
    above, below = lax.rem(gy + 1, n_gy), lax.rem(gy + n_gy - 1, n_gy)
    low_half = gy < n_gy // 2

    loads = [
        pltpu.make_async_copy(src, dst, in_sem.at[i])
        for i, (src, dst) in enumerate(((frac_h, fracv), (donor_h, donv), (state_h, stv), (cell_h, cellv)))
    ]
    for load in loads:
        load.start()

    barrier = pltpu.get_barrier_semaphore()
    for off in range(1, n_gy):
        pl.semaphore_signal(barrier, inc=1, device_id={"gy": lax.rem(gy + off, n_gy)}, device_id_type=MESH)
    for other in (left, right):
        pl.semaphore_signal(barrier, inc=1, device_id={"gx": other}, device_id_type=MESH)

    def pack(x):
        tail = x[:, 128:192]
        return x[:, 0:128], jnp.concatenate([tail[0:8], tail[8:16]], axis=1)

    loads[0].wait()
    fsend[...] = jnp.zeros_like(fsend)
    for c in range(3):
        main, tail = pack(fracv[c])
        fsend[pl.ds(c, 16, 8), :] = main
        fsend[pl.ds(3 + c, 8, 8), :] = tail
        fsend[pl.ds(64 + 3 + c, 8, 8), :] = tail
    pl.semaphore_wait(barrier, n_gy + 1)

    def exchange(send, recv, rows, s_sem, r_sem):
        copies = []
        mine = pl.ds(pl.multiple_of(gy * rows, 8), rows)
        for off in range(1, n_gy):
            other = lax.rem(gy + off, n_gy)
            copy = pltpu.make_async_remote_copy(
                src_ref=send.at[pl.ds(pl.multiple_of(other * rows, 8), rows), :],
                dst_ref=recv.at[mine, :],
                send_sem=s_sem.at[off - 1],
                recv_sem=r_sem.at[off - 1],
                device_id={"gy": other},
                device_id_type=MESH,
            )
            copy.start()
            copies.append(copy)
        recv[mine, :] = send[mine, :]
        return copies

    frac_copies = exchange(fsend, frecv, 8, fs_sem, fr_sem)

    loads[1].wait()
    main, tail = pack(donv[...])
    kq[...] = jnp.concatenate([main, tail], axis=0)
    loads[2].wait()
    flat = stv[...].reshape(240, 128)
    high = flat.astype(BF16)
    ss[:, 0:128] = high
    ss[:, 128:256] = (flat - high.astype(F32)).astype(BF16)

    def corners(r):
        donor = kq[pl.ds(r, 1), :]
        k = jnp.bitwise_and(donor, 127)
        i0 = jnp.right_shift(donor, 11)
        at = iota((128, 128), 0) - k
        here = jnp.where(at == 0, 1.0, 0.0).astype(F32)
        step = jnp.where(at == 1, 1.0, -here)
        here, step = here.astype(BF16), step.astype(BF16)
        z = jnp.concatenate(
            [jnp.concatenate([here, here], axis=0), jnp.concatenate([step, step], axis=0)], axis=1
        )
        t = jnp.dot(ss[...], z, preferred_element_type=F32)
        for c in range(2):
            tc = t[:, c * 128 : (c + 1) * 128].reshape(5, NX, NY, 128)
            x0 = jnp.where(i0 == 0, tc[:, 0], tc[:, 1])
            x1 = jnp.where(i0 == 0, tc[:, 1], tc[:, 2])
            pp[r, 2 * c] = x0
            pp[r, 2 * c + 1] = x1 - x0

    loop(ROWS, corners)

    def combine(low, high):
        lane = iota((8, 128), 1)
        return jnp.where(
            lane < 64,
            jnp.where(low_half, low, pltpu.roll(low, 64, 1)),
            jnp.where(low_half, pltpu.roll(high, 64, 1), high),
        )

    for copy in frac_copies:
        copy.wait_recv()
    for c in range(3):
        fq[c, 0:16] = frecv[pl.ds(c, 16, 8), :]
        fq[c, 16:24] = combine(frecv[pl.ds(3 + c, 8, 8), :], frecv[pl.ds(64 + 3 + c, 8, 8), :])

    def image(r):
        donor = kq[pl.ds(r, 1), :]
        j0 = jnp.bitwise_and(jnp.right_shift(donor, 7), 15)
        f0, f1, f2 = (fq[c, pl.ds(r, 1), :] for c in range(3))
        at = iota((NY, 128), 0) - j0
        wy = jnp.where(at == 0, 1.0 - f1, jnp.where(at == 1, f1, 0.0))
        value = pp[r, 0] + f0 * pp[r, 1] + f2 * (pp[r, 2] + f0 * pp[r, 3])
        return jnp.sum(value * wy, axis=1)

    def image_main(r):
        isend[pl.ds(pl.multiple_of(r * 16, 16), 5), :] = image(r)

    def image_tail(t):
        value = image(t + 16)
        isend[pl.ds(pl.multiple_of(t * 16, 16) + 8, 5), :] = value
        isend[pl.ds(pl.multiple_of(t * 16, 16) + 136, 5), :] = value

    isend[...] = jnp.zeros_like(isend)
    loop(16, image_main)
    loop(8, image_tail)
    image_copies = exchange(isend, irecv, 16, is_sem, ir_sem)

    loads[3].wait()
    main, tail = pack(cellv[...])
    valid = jnp.concatenate([main, tail], axis=0)
    cq[...] = jnp.where(valid < 0, -4096, valid)

    def places(r):
        cell = cq[pl.ds(r, 1), :]
        j = jnp.right_shift(cell, 7)
        column = jnp.bitwise_or(jnp.bitwise_and(jnp.right_shift(cell, 3), 128), jnp.bitwise_and(cell, 127))
        row = jnp.bitwise_or(jnp.left_shift(jnp.right_shift(cell, 11), 3), jnp.bitwise_and(j, 7))
        bs[:, pl.ds(pl.multiple_of(r * 128, 128), 128)] = jnp.where(iota((256, 128), 0) == column, 1.0, 0.0).astype(BF16)
        i48 = iota((48, 128), 0)
        want = jnp.bitwise_or(jnp.left_shift(jnp.right_shift(i48, 4), 3), jnp.bitwise_and(i48, 7))
        ohs[:, pl.ds(pl.multiple_of(r * 128, 128), 128)] = jnp.where(want == row, 1.0, 0.0).astype(BF16)

    loop(ROWS, places)
    nt = (((1,), (1,)), ((), ()))
    count = lax.dot_general(ohs[...], bs[...], nt, preferred_element_type=F32).reshape(NX, 2, 8, 256)
    maskv[:, 0:8] = count[:, 0, :, 0:128]
    maskv[:, 8:16] = count[:, 0, :, 128:256]

    for copy in image_copies:
        copy.wait_recv()

    def spread(ghost, r):
        where = pl.ds(r * 128, 128)
        rows = ohs[:, where].reshape(NX, 16, 128)
        for v in range(5):
            g = jnp.broadcast_to(SIGN[v] * ghost[v], (8, 128))
            hi = g.astype(BF16)
            lo = (g - hi.astype(F32)).astype(BF16)
            both = jnp.concatenate([hi, lo], axis=0)
            am[v * 48 : (v + 1) * 48, where] = (rows * both[None]).reshape(48, 128)

    for r in range(16):
        spread([irecv[r * 16 + v : r * 16 + v + 1, :] for v in range(5)], r)
    for t in range(8):
        value = combine(irecv[t * 16 + 8 : t * 16 + 16, :], irecv[t * 16 + 136 : t * 16 + 144, :])
        spread([value[v : v + 1] for v in range(5)], 16 + t)
    ghost = lax.dot_general(am[...], bs[...], nt, preferred_element_type=F32).reshape(5, NX, 2, 8, 256)
    ghost = ghost[:, :, 0] + ghost[:, :, 1]
    for half in range(2):
        rows = pl.ds(half * 8, 8)
        fil[:, :, rows] = jnp.where(
            maskv[:, rows][None] > 0.5, ghost[..., half * 128 : (half + 1) * 128], stv[:, :, rows]
        )

    halo_copies = []
    for i, (src, dst, where) in enumerate(
        (
            (fil, xl, {"gx": right}),
            (fil, xr, {"gx": left}),
            (fil.at[:, :, 8:16, :], yl, {"gy": above}),
            (fil.at[:, :, 0:8, :], yr, {"gy": below}),
        )
    ):
        copy = pltpu.make_async_remote_copy(
            src_ref=src, dst_ref=dst, send_sem=hs_sem.at[i], recv_sem=hr_sem.at[i], device_id=where, device_id_type=MESH
        )
        copy.start()
        halo_copies.append(copy)

    u = [fil[v] for v in range(5)]
    rinv, p = inverse_pressure(u)
    for v, pair in enumerate(split(u, rinv, p, 2, lf[2])):
        for s in range(2):
            fz[s, v * NX : (v + 1) * NX] = pair[s]
    for v, pair in enumerate(split(u, rinv, p, 1, lf[1])):
        for s in range(2):
            for i in range(NX):
                fy[pl.ds((s * 32 + 8) * 16 + v * NX + i, 16, 16), :] = pair[s][i]
    for v, pair in enumerate(split(u, rinv, p, 0, lf[0])):
        for s in range(2):
            fx[s, v, 3:6] = pair[s]

    def along_z(n):
        chg[n] = z_change(fz[0, n], fz[1, n])

    loop(15, along_z)

    for copy in halo_copies[2:]:
        copy.wait_recv()
    for edge, ref, row, base in ((gy == 0, yl, 0, 0), (gy == n_gy - 1, yr, 15, 24)):
        u = [jnp.where(edge, fil[v, :, row : row + 1, :], ref[v]) for v in range(5)]
        rinv, p = inverse_pressure(u)
        for v, pair in enumerate(split(u, rinv, p, 1, lf[1])):
            for s in range(2):
                for i in range(NX):
                    fy[pl.ds((s * 32 + base) * 16 + v * NX + i, 8, 16), :] = pair[s][i]

    def along_y(n):
        b, h = n // 2, n % 2

        def window(s, start, count):
            return jnp.stack([fy[pl.ds(pl.multiple_of((s * 32 + start + q) * 16 + h * 8, 8), 8), :] for q in range(count)])

        flux = upwind(*betas(window(0, 5 + 3 * b, 7))) + downwind(*betas(window(1, 6 + 3 * b, 7)))
        for q in range(3):
            fluxy[pl.ds(pl.multiple_of((3 * b + q) * 16 + h * 8, 8), 8), :] = flux[q]

    loop(12, along_y)
    for n in range(15):
        chg[n] = chg[n] + (fluxy[pl.ds(16 + n, 16, 16), :] - fluxy[pl.ds(n, 16, 16), :])

    for copy in halo_copies[:2]:
        copy.wait_recv()
    for edge, ref, row, base in ((gx == 0, xl, 0, 0), (gx == n_gx - 1, xr, 2, 6)):
        u = [jnp.where(edge, fil[v, row : row + 1], ref[v]) for v in range(5)]
        rinv, p = inverse_pressure(u)
        for v, pair in enumerate(split(u, rinv, p, 0, lf[0])):
            for s in range(2):
                fx[s, v, base : base + 3] = pair[s]

    def along_x(n):
        v, h = n // 2, n % 2
        rows = pl.ds(pl.multiple_of(h * 8, 8), 8)
        flux = upwind(*betas(fx[0, v, 0:8, rows])) + downwind(*betas(fx[1, v, 1:9, rows]))
        change = flux[1:] - flux[:-1] + chg[pl.ds(v * NX, NX), rows]
        mine = fil[v, :, rows]
        outv[v, :, rows] = jnp.where(maskv[:, rows] > 0.5, mine, mine - (0.125 / 6.0) * change)

    loop(10, along_x)
    store = pltpu.make_async_copy(outv, out_h, out_sem)
    store.start()
    for copy in frac_copies + image_copies + halo_copies:
        copy.wait_send()
    store.wait()


def solution(mesh):
    n_gx, n_gy = mesh.shape["gx"], mesh.shape["gy"]

    def on_device(state, lf_speed, ghost_cell, ghost_frac, donor_block):
        hbm = pl.BlockSpec(memory_space=pl.ANY)
        vmem = pltpu.VMEM
        dma = pltpu.SemaphoreType.DMA
        brick = (5, NX, NY, NZ)
        return pl.pallas_call(
            functools.partial(kernel, n_gx, n_gy),
            out_shape=jax.ShapeDtypeStruct(brick, F32),
            in_specs=[pl.BlockSpec(memory_space=pltpu.SMEM), hbm, hbm, hbm, hbm],
            out_specs=hbm,
            scratch_shapes=[
                vmem(brick, F32),
                vmem((16, 192), jnp.int32),
                vmem((3, 16, 192), F32),
                vmem((16, 192), jnp.int32),
                vmem((128, 128), F32),
                vmem((128, 128), F32),
                vmem((256, 128), F32),
                vmem((256, 128), F32),
                vmem((ROWS, 128), jnp.int32),
                vmem((ROWS, 128), jnp.int32),
                vmem((3, ROWS, 128), F32),
                vmem((240, 256), BF16),
                vmem((ROWS, 4, 5, NY, 128), F32),
                vmem((256, ROWS * 128), BF16),
                vmem((48, ROWS * 128), BF16),
                vmem((240, ROWS * 128), BF16),
                vmem((NX, NY, NZ), F32),
                vmem(brick, F32),
                vmem(brick, F32),
                vmem(brick, F32),
                vmem((5, NX, 8, NZ), F32),
                vmem((5, NX, 8, NZ), F32),
                vmem((2, 5, 9, NY, NZ), F32),
                vmem((2 * 32 * 16, NZ), F32),
                vmem((2, 15, NY, NZ), F32),
                vmem((18 * 16, NZ), F32),
                vmem((15, NY, NZ), F32),
                vmem(brick, F32),
                dma((4,)),
                dma((n_gy - 1,)),
                dma((n_gy - 1,)),
                dma((n_gy - 1,)),
                dma((n_gy - 1,)),
                dma((4,)),
                dma((4,)),
                dma,
            ],
            compiler_params=pltpu.CompilerParams(
                collective_id=0, has_side_effects=True, vmem_limit_bytes=48 * 1024 * 1024
            ),
        )(
            lf_speed,
            state,
            ghost_cell.reshape(ghost_cell.shape[2:]),
            ghost_frac.reshape((3,) + ghost_frac.shape[3:]),
            donor_block.reshape(donor_block.shape[2:]),
        )

    return jax.shard_map(
        on_device,
        mesh=mesh,
        in_specs=(
            P(None, "gx", "gy", None),
            P(),
            P("gx", "gy", None, None),
            P(None, "gx", "gy", None, None),
            P("gx", "gy", None, None),
        ),
        out_specs=P(None, "gx", "gy", None),
        check_vma=False,
    )
```

time: 237 us -> 48.7 us (0.21)
  the two profiles are of different devices: /device:TPU:15 before, /device:TPU:1 now
where the time goes in v1:
time: 48.7 us; the launch traced here: 48.4 us
  Pallas kernels  44 us (90%)
  local copies, waits for them, and re-layouts  4.44 us (9%)
    pallas_call x1, Pallas kernels, on_device(): pl.pallas_call(functools.partial(kernel, n_gx, n_gy), out_shape=jax.Shape...  44 us
    unnamed x11, local copies, waits for them, and re-layouts  4.44 us

profile of v1, /device:TPU:1, one launch (start us, length us, event | category | flops | bytes accessed | tf_op | source)
XLA Modules:
  0.0 48.4 jit_solution(458892192356607341)
XLA Ops:
  0.0 0.0 copy-start.4
  0.0 0.7 %copy-done.4 = f32[3]{0:T(128)S(1)} copy-done((f32[3]{0:T(128)S(1)}, f32[3]{0:T(128)}, u32[]{:S(2)}) %copy-start.4) | copy-done | bytes 36
  0.7 0.0 copy-start
  0.7 0.9 %copy-done = f32[5,3,16,128]{3,2,1,0:T(8,128)S(1)} copy-done((f32[5,3,16,128]{3,2,1,0:T(8,128)S(1)}, f32[5,3,16,128]{3,2,1,0:T(8,128)}, u32[]{:S(2)}) %copy-start) | copy-done | bytes 122904
  1.6 0.0 copy-start.1
  1.6 0.8 %copy-done.1 = f32[3,1,1,16,192]{4,3,2,1,0:T(8,128)S(1)} copy-done((f32[3,1,1,16,192]{4,3,2,1,0:T(8,128)S(1)}, f32[3,1,1,16,192]{4,3,2,1,0:T(8,128)}, u32[]{:S(2)}) %copy-start.1) | copy-done | bytes 36888
  2.4 0.0 copy-start.2
  2.4 0.7 %copy-done.2 = s32[1,1,16,192]{3,2,1,0:T(8,128)S(1)} copy-done((s32[1,1,16,192]{3,2,1,0:T(8,128)S(1)}, s32[1,1,16,192]{3,2,1,0:T(8,128)}, u32[]{:S(2)}) %copy-start.2) | copy-done | bytes 12312
  3.1 0.0 copy-start.3
  3.1 0.7 %copy-done.3 = s32[1,1,16,192]{3,2,1,0:T(8,128)S(1)} copy-done((s32[1,1,16,192]{3,2,1,0:T(8,128)S(1)}, s32[1,1,16,192]{3,2,1,0:T(8,128)}, u32[]{:S(2)}) %copy-start.3) | copy-done | bytes 12312
  3.8 44.0 %shard_map.55 = f32[5,3,16,128]{3,2,1,0:T(8,128)S(1)} custom-call(f32[3]{0:T(128)S(1)} %copy-done.4, f32[5,3,16,128]{3,2,1,0:T(8,128)S(1)} %copy-done, s32[16,192]{1,0:T(8,128)S(1)} %bitcast.4, f32[3,16,192]{2,1,0:T(8,128)S(1)} %bitcast.3, s32[16,192]{1,0:T(8,128)S(1)} %bitcast.5), custom_call_target="tpu_custom_call" | custom-call | tf_op jit(solution)/shard_map/pallas_call | solution.py:374
  47.8 0.7 %copy.7 = f32[5,3,16,128]{3,2,1,0:T(8,128)} copy(f32[5,3,16,128]{3,2,1,0:T(8,128)S(1)} %shard_map.55) | data formatting | bytes 245760
Async XLA Ops:
  0.0 0.7 %copy-start.4 = (f32[3]{0:T(128)S(1)}, f32[3]{0:T(128)}, u32[]{:S(2)}) copy-start(f32[3]{0:T(128)} %lf.1) | copy-start | bytes 40
  0.7 0.9 %copy-start = (f32[5,3,16,128]{3,2,1,0:T(8,128)S(1)}, f32[5,3,16,128]{3,2,1,0:T(8,128)}, u32[]{:S(2)}) copy-start(f32[5,3,16,128]{3,2,1,0:T(8,128)} %state_h.1) | copy-start | bytes 368644
  1.6 0.8 %copy-start.1 = (f32[3,1,1,16,192]{4,3,2,1,0:T(8,128)S(1)}, f32[3,1,1,16,192]{4,3,2,1,0:T(8,128)}, u32[]{:S(2)}) copy-start(f32[3,1,1,16,192]{4,3,2,1,0:T(8,128)} %param.8) | copy-start | bytes 110596
  2.4 0.7 %copy-start.2 = (s32[1,1,16,192]{3,2,1,0:T(8,128)S(1)}, s32[1,1,16,192]{3,2,1,0:T(8,128)}, u32[]{:S(2)}) copy-start(s32[1,1,16,192]{3,2,1,0:T(8,128)} %param.7) | copy-start | bytes 36868
  3.1 0.7 %copy-start.3 = (s32[1,1,16,192]{3,2,1,0:T(8,128)S(1)}, s32[1,1,16,192]{3,2,1,0:T(8,128)}, u32[]{:S(2)}) copy-start(s32[1,1,16,192]{3,2,1,0:T(8,128)} %param.9) | copy-start | bytes 36868

commit v2 on v1

--- a/solution.py
+++ b/solution.py
@@ -112,46 +112,70 @@
 
 
 def kernel(
-    n_gx, n_gy, lf, state_h, cell_h, frac_h, donor_h, out_h,
+    n_gx, n_gy, lf_h, state_h, cell_h, frac_h, donor_h, out_h,
     stv, cellv, fracv, donv, fsend, frecv, isend, irecv, kq, cq, fq, ss, pp, bs, ohs, am, maskv,
-    fil, xl, xr, yl, yr, fx, fy, fz, fluxy, chg, outv,
+    fil, xl, xr, yl, yr, fx, fy, fz, fluxy, chg, outv, lf,
     in_sem, fs_sem, fr_sem, is_sem, ir_sem, hs_sem, hr_sem, out_sem,
 ):
     gx, gy = lax.axis_index("gx"), lax.axis_index("gy")
-    right, left = lax.rem(gx + 1, n_gx), lax.rem(gx + n_gx - 1, n_gx)
-    above, below = lax.rem(gy + 1, n_gy), lax.rem(gy + n_gy - 1, n_gy)
-    low_half = gy < n_gy // 2
+    right, left, above, below = gx + 1, gx - 1, gy + 1, gy - 1
+    has_left, has_right, has_below, has_above = gx > 0, gx < n_gx - 1, gy > 0, gy < n_gy - 1
+    half = iota((1, 128), 1) < 64
 
     loads = [
         pltpu.make_async_copy(src, dst, in_sem.at[i])
-        for i, (src, dst) in enumerate(((frac_h, fracv), (donor_h, donv), (state_h, stv), (cell_h, cellv)))
+        for i, (src, dst) in enumerate(((frac_h, fracv), (donor_h, donv), (state_h, stv), (cell_h, cellv), (lf_h, lf)))
     ]
     for load in loads:
         load.start()
 
     barrier = pltpu.get_barrier_semaphore()
-    for off in range(1, n_gy):
+    for off in sorted(range(1, n_gy), key=lambda off: -min(off, n_gy - off)):
         pl.semaphore_signal(barrier, inc=1, device_id={"gy": lax.rem(gy + off, n_gy)}, device_id_type=MESH)
-    for other in (left, right):
-        pl.semaphore_signal(barrier, inc=1, device_id={"gx": other}, device_id_type=MESH)
+    for inside, other in ((has_left, left), (has_right, right)):
+
+        @pl.when(inside)
+        def _():
+            pl.semaphore_signal(barrier, inc=1, device_id={"gx": other}, device_id_type=MESH)
+
 
     def pack(x):
         tail = x[:, 128:192]
         return x[:, 0:128], jnp.concatenate([tail[0:8], tail[8:16]], axis=1)
 
+    def turn(x):
+        return pltpu.roll(x, 64, 1)
+
+    def share(tails):
+        low = [jnp.where(half, a, turn(b)) for a, b in zip(tails[0::2], tails[1::2])]
+        high = [jnp.where(half, turn(a), b) for a, b in zip(tails[0::2], tails[1::2])]
+        return low + [tails[-1]], high + [turn(tails[-1])]
+
+    def unshare(low, high):
+        rows = []
+        for a, b in zip(low, high):
+            rows += [jnp.where(half, a, turn(b)), jnp.where(half, turn(a), b)]
+        return rows[:-1]
+
     loads[0].wait()
     fsend[...] = jnp.zeros_like(fsend)
+    tails = []
     for c in range(3):
         main, tail = pack(fracv[c])
         fsend[pl.ds(c, 16, 8), :] = main
-        fsend[pl.ds(3 + c, 8, 8), :] = tail
-        fsend[pl.ds(64 + 3 + c, 8, 8), :] = tail
-    pl.semaphore_wait(barrier, n_gy + 1)
+        tails.append(tail)
+    low, high = share(tails)
+    for c in range(2):
+        fsend[pl.ds(3 + c, 8, 8), :] = low[c]
+        fsend[pl.ds(64 + 3 + c, 8, 8), :] = high[c]
+    pl.semaphore_wait(barrier, n_gy - 1 + has_left.astype(jnp.int32) + has_right.astype(jnp.int32))
+
+    far = sorted(range(1, n_gy), key=lambda off: -min(off, n_gy - off))
 
     def exchange(send, recv, rows, s_sem, r_sem):
         copies = []
         mine = pl.ds(pl.multiple_of(gy * rows, 8), rows)
-        for off in range(1, n_gy):
+        for off in far:
             other = lax.rem(gy + off, n_gy)
             copy = pltpu.make_async_remote_copy(
                 src_ref=send.at[pl.ds(pl.multiple_of(other * rows, 8), rows), :],
@@ -198,19 +222,15 @@
 
     loop(ROWS, corners)
 
-    def combine(low, high):
-        lane = iota((8, 128), 1)
-        return jnp.where(
-            lane < 64,
-            jnp.where(low_half, low, pltpu.roll(low, 64, 1)),
-            jnp.where(low_half, pltpu.roll(high, 64, 1), high),
-        )
-
     for copy in frac_copies:
         copy.wait_recv()
     for c in range(3):
         fq[c, 0:16] = frecv[pl.ds(c, 16, 8), :]
-        fq[c, 16:24] = combine(frecv[pl.ds(3 + c, 8, 8), :], frecv[pl.ds(64 + 3 + c, 8, 8), :])
+    tails = unshare(
+        [frecv[pl.ds(3 + c, 8, 8), :] for c in range(2)], [frecv[pl.ds(67 + c, 8, 8), :] for c in range(2)]
+    )
+    for c in range(3):
+        fq[c, 16:24] = tails[c]
 
     def image(r):
         donor = kq[pl.ds(r, 1), :]
@@ -222,19 +242,21 @@
         return jnp.sum(value * wy, axis=1)
 
     def image_main(r):
-        isend[pl.ds(pl.multiple_of(r * 16, 16), 5), :] = image(r)
+        isend[pl.ds(pl.multiple_of(r * 8, 8), 5), :] = image(r)
 
     def image_tail(t):
         value = image(t + 16)
-        isend[pl.ds(pl.multiple_of(t * 16, 16) + 8, 5), :] = value
-        isend[pl.ds(pl.multiple_of(t * 16, 16) + 136, 5), :] = value
-
-    isend[...] = jnp.zeros_like(isend)
+        low, high = share([value[v : v + 1] for v in range(5)])
+        for c in range(3):
+            isend[pl.ds(pl.multiple_of(t * 8, 8) + 5 + c, 1), :] = low[c]
+            isend[pl.ds(pl.multiple_of(t * 8, 8) + 69 + c, 1), :] = high[c]
+
     loop(16, image_main)
     loop(8, image_tail)
-    image_copies = exchange(isend, irecv, 16, is_sem, ir_sem)
+    image_copies = exchange(isend, irecv, 8, is_sem, ir_sem)
 
     loads[3].wait()
+    loads[4].wait()
     main, tail = pack(cellv[...])
     valid = jnp.concatenate([main, tail], axis=0)
     cq[...] = jnp.where(valid < 0, -4096, valid)
@@ -269,10 +291,10 @@
             am[v * 48 : (v + 1) * 48, where] = (rows * both[None]).reshape(48, 128)
 
     for r in range(16):
-        spread([irecv[r * 16 + v : r * 16 + v + 1, :] for v in range(5)], r)
+        spread([irecv[r * 8 + v : r * 8 + v + 1, :] for v in range(5)], r)
     for t in range(8):
-        value = combine(irecv[t * 16 + 8 : t * 16 + 16, :], irecv[t * 16 + 136 : t * 16 + 144, :])
-        spread([value[v : v + 1] for v in range(5)], 16 + t)
+        low, high = ([irecv[b + 5 + c : b + 6 + c, :] for c in range(3)] for b in (t * 8, t * 8 + 64))
+        spread(unshare(low, high), 16 + t)
     ghost = lax.dot_general(am[...], bs[...], nt, preferred_element_type=F32).reshape(5, NX, 2, 8, 256)
     ghost = ghost[:, :, 0] + ghost[:, :, 1]
     for half in range(2):
@@ -281,20 +303,30 @@
             maskv[:, rows][None] > 0.5, ghost[..., half * 128 : (half + 1) * 128], stv[:, :, rows]
         )
 
-    halo_copies = []
-    for i, (src, dst, where) in enumerate(
-        (
-            (fil, xl, {"gx": right}),
-            (fil, xr, {"gx": left}),
-            (fil.at[:, :, 8:16, :], yl, {"gy": above}),
-            (fil.at[:, :, 0:8, :], yr, {"gy": below}),
+    halos = {
+        name: (
+            pltpu.make_async_remote_copy(
+                src_ref=src, dst_ref=dst, send_sem=hs_sem.at[i], recv_sem=hr_sem.at[i], device_id=where, device_id_type=MESH
+            ),
+            sends,
+            receives,
         )
-    ):
-        copy = pltpu.make_async_remote_copy(
-            src_ref=src, dst_ref=dst, send_sem=hs_sem.at[i], recv_sem=hr_sem.at[i], device_id=where, device_id_type=MESH
+        for i, (name, src, dst, where, sends, receives) in enumerate(
+            (
+                ("xl", fil, xl, {"gx": right}, has_right, has_left),
+                ("xr", fil, xr, {"gx": left}, has_left, has_right),
+                ("yl", fil.at[:, :, 8:16, :], yl, {"gy": above}, has_above, has_below),
+                ("yr", fil.at[:, :, 0:8, :], yr, {"gy": below}, has_below, has_above),
+            )
         )
-        copy.start()
-        halo_copies.append(copy)
+    }
+    for copy, sends, _ in halos.values():
+        pl.when(sends)(copy.start)
+
+    def arrived(*names):
+        for name in names:
+            copy, _, receives = halos[name]
+            pl.when(receives)(copy.wait_recv)
 
     u = [fil[v] for v in range(5)]
     rinv, p = inverse_pressure(u)
@@ -314,9 +346,8 @@
 
     loop(15, along_z)
 
-    for copy in halo_copies[2:]:
-        copy.wait_recv()
-    for edge, ref, row, base in ((gy == 0, yl, 0, 0), (gy == n_gy - 1, yr, 15, 24)):
+    arrived("yl", "yr")
+    for edge, ref, row, base in ((~has_below, yl, 0, 0), (~has_above, yr, 15, 24)):
         u = [jnp.where(edge, fil[v, :, row : row + 1, :], ref[v]) for v in range(5)]
         rinv, p = inverse_pressure(u)
         for v, pair in enumerate(split(u, rinv, p, 1, lf[1])):
@@ -338,9 +369,8 @@
     for n in range(15):
         chg[n] = chg[n] + (fluxy[pl.ds(16 + n, 16, 16), :] - fluxy[pl.ds(n, 16, 16), :])
 
-    for copy in halo_copies[:2]:
-        copy.wait_recv()
-    for edge, ref, row, base in ((gx == 0, xl, 0, 0), (gx == n_gx - 1, xr, 2, 6)):
+    arrived("xl", "xr")
+    for edge, ref, row, base in ((~has_left, xl, 0, 0), (~has_right, xr, 2, 6)):
         u = [jnp.where(edge, fil[v, row : row + 1], ref[v]) for v in range(5)]
         rinv, p = inverse_pressure(u)
         for v, pair in enumerate(split(u, rinv, p, 0, lf[0])):
@@ -358,8 +388,10 @@
     loop(10, along_x)
     store = pltpu.make_async_copy(outv, out_h, out_sem)
     store.start()
-    for copy in frac_copies + image_copies + halo_copies:
+    for copy in frac_copies + image_copies:
         copy.wait_send()
+    for copy, sends, _ in halos.values():
+        pl.when(sends)(copy.wait_send)
     store.wait()
 
 
@@ -374,7 +406,7 @@
         return pl.pallas_call(
             functools.partial(kernel, n_gx, n_gy),
             out_shape=jax.ShapeDtypeStruct(brick, F32),
-            in_specs=[pl.BlockSpec(memory_space=pltpu.SMEM), hbm, hbm, hbm, hbm],
+            in_specs=[hbm] * 5,
             out_specs=hbm,
             scratch_shapes=[
                 vmem(brick, F32),
@@ -383,8 +415,8 @@
                 vmem((16, 192), jnp.int32),
                 vmem((128, 128), F32),
                 vmem((128, 128), F32),
-                vmem((256, 128), F32),
-                vmem((256, 128), F32),
+                vmem((128, 128), F32),
+                vmem((128, 128), F32),
                 vmem((ROWS, 128), jnp.int32),
                 vmem((ROWS, 128), jnp.int32),
                 vmem((3, ROWS, 128), F32),
@@ -405,7 +437,8 @@
                 vmem((18 * 16, NZ), F32),
                 vmem((15, NY, NZ), F32),
                 vmem(brick, F32),
-                dma((4,)),
+                pltpu.SMEM((3,), F32),
+                dma((5,)),
                 dma((n_gy - 1,)),
                 dma((n_gy - 1,)),
                 dma((n_gy - 1,)),
@@ -415,7 +448,7 @@
                 dma,
             ],
             compiler_params=pltpu.CompilerParams(
-                collective_id=0, has_side_effects=True, vmem_limit_bytes=48 * 1024 * 1024
+                collective_id=0, has_side_effects=True, vmem_limit_bytes=63 * 1024 * 1024
             ),
         )(
             lf_speed,

time: 48.7 us -> 41.3 us (0.85)
  the two profiles are of different devices: /device:TPU:1 before, /device:TPU:15 now
where the time goes in v2:
time: 41.3 us; the launch traced here: 40.9 us
  Pallas kernels  39.3 us (95%)
  local copies, waits for them, and re-layouts  1.56 us (4%)
    pallas_call x1, Pallas kernels, on_device(): pl.pallas_call(functools.partial(kernel, n_gx, n_gy), out_shape=jax.Shape...  39.3 us
    unnamed x1, local copies, waits for them, and re-layouts  1.56 us

profile of v2, /device:TPU:15, one launch (start us, length us, event | category | flops | bytes accessed | tf_op | source)
XLA Modules:
  0.0 40.9 jit_solution(4596753017125412523)
XLA Ops:
  0.0 39.3 %shard_map.55 = f32[5,3,16,128]{3,2,1,0:T(8,128)} custom-call(f32[3]{0:T(128)} %lf_h.1, f32[5,3,16,128]{3,2,1,0:T(8,128)} %state_h.1, s32[16,192]{1,0:T(8,128)} %bitcast.4, f32[3,16,192]{2,1,0:T(8,128)} %bitcast.3, s32[16,192]{1,0:T(8,128)} %bitcast.5), custom_call_target="tpu_custom_call" | custom-call | tf_op jit(solution)/shard_map/pallas_call | solution.py:406
  39.3 1.6 %copy.7 = f32[5,3,16,128]{3,2,1,0:T(8,128)} copy(f32[5,3,16,128]{3,2,1,0:T(8,128)} %shard_map.55) | data formatting | bytes 245760

commit v3 on v2

v3 whole, which is shorter than its diff:
```python
import functools

import jax
import jax.numpy as jnp
from jax import lax
from jax.experimental import pallas as pl
from jax.experimental.pallas import tpu as pltpu
from jax.sharding import PartitionSpec as P

MESH = pl.DeviceIdType.MESH
F32 = jnp.float32
BF16 = jnp.bfloat16
SIGN = (1.0, -1.0, -1.0, -1.0, 1.0)
EPS = 16.0e-6
C13 = 13.0 / 3.0
NX, NY, NZ = 3, 16, 128
ROWS = 24


def loop(count, body):
    def step(i, carry):
        body(i)
        return carry

    lax.fori_loop(0, count, step, 0, unroll=True)


def sq(x):
    return x * x


def rcp(x):
    r = pl.reciprocal(x, approx=True)
    return r * (2.0 - x * r)


def iota(shape, dim):
    return lax.broadcasted_iota(jnp.int32, shape, dim)


def betas(w):
    n = w.shape[0] - 4
    d = w[1:] - w[:-1]
    dd = d[1:] - d[:-1]
    e = (C13 * dd) * dd + EPS
    t = dd[1:] - dd[:-1]
    left = e[:n] + sq(3.0 * d[1 : n + 1] - d[:n])
    mid = e[1 : n + 1] + sq(d[1 : n + 1] + d[2 : n + 2])
    right = e[2 : n + 2] + sq(3.0 * d[2 : n + 2] - d[3 : n + 3])
    return w[2 : n + 2], d[1 : n + 1], d[2 : n + 2], t[:n], t[1:], left, mid, right


def upwind(f, dm, dp, tm, tp, left, mid, right):
    a, b, c = sq(mid * right), sq(left * right), 3.0 * sq(left * mid)
    return 6.0 * f + dm + 2.0 * dp - (2.0 * a * tm + c * tp) * rcp(a + 6.0 * b + c)


def downwind(f, dm, dp, tm, tp, left, mid, right):
    a, b, c = sq(mid * left), sq(left * right), 3.0 * sq(mid * right)
    return 6.0 * f - dp - 2.0 * dm + (2.0 * a * tp + c * tm) * rcp(a + 6.0 * b + c)


def z_change(fp, fm):
    lane = iota(fp.shape, 1)
    first, last = lane == 0, lane == NZ - 1
    down = lambda x: pltpu.roll(x, 1, 1)
    up = lambda x: pltpu.roll(x, NZ - 1, 1)

    def parts(f):
        dp = jnp.where(last, 0.0, up(f) - f)
        dm = down(dp)
        dd = dp - dm
        e = (C13 * dd) * dd + EPS
        left, right = e + sq(3.0 * dp - dm), e + sq(3.0 * dm - dp)
        mid = e + sq(dp + dm)
        tm = dd - jnp.where(first, 0.0, down(dd))
        tp = jnp.where(last, 0.0, up(dd)) - dd
        args = (f, dm, dp, tm, tp, jnp.where(first, EPS, down(left)), mid, jnp.where(last, EPS, up(right)))
        return args, dd, left, right

    plus, dd_plus, _, right = parts(fp)
    minus, dd_minus, left, _ = parts(fm)
    rp, rm = upwind(*plus), downwind(*minus)
    f = jnp.where(first, fp, fm)
    dd = jnp.where(first, dd_plus, dd_minus)
    far = jnp.where(first, right, left)
    edge = 6.0 * f - 3.0 * EPS * EPS * dd * rcp(7.0 * sq(far) + 3.0 * EPS * EPS)
    return rp - jnp.where(first, edge, down(rp)) + jnp.where(last, edge, up(rm)) - rm


def inverse_pressure(u):
    rinv = 1.0 / u[0]
    kinetic = (u[1] * u[1] + u[2] * u[2] + u[3] * u[3]) * rinv
    return rinv, 0.4 * (u[4] - 0.5 * kinetic)


def split(u, rinv, p, direction, speed):
    normal = u[1 + direction] * rinv
    result = []
    for v in range(5):
        if v == 0:
            f = u[1 + direction]
        elif v == 4:
            f = normal * (u[4] + p)
        else:
            f = normal * u[v]
            if v == 1 + direction:
                f = f + p
        s = speed * u[v]
        result.append((f + s, f - s))
    return result


OTHER = [8, 15, 14, 13, 12, 11, 10, 9]
NEAR = [0, 1, 2, 3, 4, 5, 11, 12, 13, 14, 15, 16 + 1, 16 + 2, 16 + 3, 16 + 4, 16 + 5]
FAR = [6, 7, 8, 9, 10, 16 + 6, 16 + 7, 16 + 0]
ORDER = NEAR + FAR
PLACE = {row: place for place, row in enumerate(ORDER)}
PARTS = (slice(0, 6), slice(11, 16), slice(6, 11))


def kernel(
    n_gx, n_gy, lf_h, state_h, cell_h, frac_h, donor_h, out,
    stv, cellv, fracv, donv, fsend, frecv, isend, irecv, kq, cq, ss, pp, bs, ohs, am, maskv, part,
    fil, yl, yr, fx, fy, fz, fluxy, chg, lf,
    in_sem, fs_sem, fr_sem, is_sem, ir_sem, hs_sem, hr_sem, xs_sem, xr_sem,
):
    gx, gy = lax.axis_index("gx"), lax.axis_index("gy")
    right, left, above, below = gx + 1, gx - 1, gy + 1, gy - 1
    has_left, has_right, has_below, has_above = gx > 0, gx < n_gx - 1, gy > 0, gy < n_gy - 1
    half = iota((1, 128), 1) < 64

    loads = [
        pltpu.make_async_copy(src, dst, in_sem.at[i])
        for i, (src, dst) in enumerate(
            ((frac_h, fracv), (donor_h, donv), (state_h, stv.at[0]), (cell_h, cellv), (lf_h, lf))
        )
    ]
    for load in loads:
        load.start()

    def partner(off):
        return lax.rem(gy + off, n_gy)

    barrier = pltpu.get_barrier_semaphore()
    for off in sorted(range(1, n_gy), key=lambda off: -min(off, n_gy - off)):
        pl.semaphore_signal(barrier, inc=1, device_id={"gy": partner(off)}, device_id_type=MESH)
    for inside, other in ((has_left, left), (has_right, right)):

        @pl.when(inside)
        def _():
            pl.semaphore_signal(barrier, inc=1, device_id={"gx": other}, device_id_type=MESH)

    def turn(x):
        return pltpu.roll(x, 64, x.ndim - 1)

    def share(tails):
        low = [jnp.where(half, a, turn(b)) for a, b in zip(tails[0::2], tails[1::2])]
        high = [jnp.where(half, turn(a), b) for a, b in zip(tails[0::2], tails[1::2])]
        return low + [tails[-1]], high + [turn(tails[-1])]

    def unshare(low, high):
        rows = []
        for a, b in zip(low, high):
            rows += [jnp.where(half, a, turn(b)), jnp.where(half, turn(a), b)]
        return rows[:-1]

    def by_distance(ref, *lead):
        rows = jnp.concatenate([ref[(*lead, pl.ds(partner(off), 1))] for off in range(16)], axis=0)
        tail = rows[:, 128:192]
        high = jnp.concatenate([tail[off : off + 1] for off in OTHER], axis=0)
        return rows[:, 0:128], jnp.concatenate([tail[0:8], high], axis=1)

    loads[0].wait()
    fsend[...] = jnp.zeros_like(fsend)
    tails = []
    for c in range(3):
        main, tail = by_distance(fracv, c)
        fsend[pl.ds(c, 16, 8), :] = main
        tails.append(tail)
    low, high = share(tails)
    for c in range(2):
        fsend[pl.ds(3 + c, 8, 8), :] = low[c]
        for t, off in enumerate(OTHER):
            fsend[off * 8 + 3 + c : off * 8 + 4 + c, :] = high[c][t : t + 1]
    pl.semaphore_wait(barrier, n_gy - 1 + has_left.astype(jnp.int32) + has_right.astype(jnp.int32))

    def message(send, recv, off, s_sem, r_sem):
        copy = pltpu.make_async_remote_copy(
            src_ref=send.at[pl.ds(off * 8, 8), :],
            dst_ref=recv.at[pl.ds((n_gy - off) * 8, 8), :],
            send_sem=s_sem.at[off - 1],
            recv_sem=r_sem.at[n_gy - off - 1],
            device_id={"gy": partner(off)},
            device_id_type=MESH,
        )
        copy.start()
        return copy

    def from_source(copies):
        return {n_gy - off: copy for off, copy in copies.items()}

    offs = [off for t in (0, 7, 6, 5, 4, 3, 2, 1) for off in (OTHER[t], t) if off]
    frac_copies = {off: message(fsend, frecv, off, fs_sem, fr_sem) for off in offs}
    frecv[0:8] = fsend[0:8]

    def beside(src, dsts, i):
        result = []
        for side, (other, sends, receives) in enumerate(((right, has_right, has_left), (left, has_left, has_right))):
            copy = pltpu.make_async_remote_copy(
                src_ref=src,
                dst_ref=dsts[side],
                send_sem=xs_sem.at[2 * i + side],
                recv_sem=xr_sem.at[2 * i + side],
                device_id={"gx": other},
                device_id_type=MESH,
            )
            pl.when(sends)(copy.start)
            result.append((copy, sends, receives))
        return result

    def arrived(copies):
        for copy, _, receives in copies:
            pl.when(receives)(copy.wait_recv)

    loads[3].wait()
    loads[2].wait()
    main, tail = by_distance(cellv)
    packed = jnp.concatenate([main, tail], axis=0)
    cq[0] = jnp.where(packed < 0, -4096, packed)
    list_copies = beside(cq.at[0], [cq.at[1], cq.at[2]], 0)

    loads[1].wait()
    main, tail = by_distance(donv)
    kq[...] = jnp.concatenate([main, tail], axis=0)
    flat = stv[0].reshape(240, 128)
    high = flat.astype(BF16)
    ss[:, 0:128] = high
    ss[:, 128:256] = (flat - high.astype(F32)).astype(BF16)

    def corners(r):
        donor = kq[pl.ds(r, 1), :]
        k = jnp.bitwise_and(donor, 127)
        i0 = jnp.right_shift(donor, 11)
        at = iota((128, 128), 0) - k
        here = jnp.where(at == 0, 1.0, 0.0).astype(F32)
        step = jnp.where(at == 1, 1.0, -here)
        here, step = here.astype(BF16), step.astype(BF16)
        z = jnp.concatenate(
            [jnp.concatenate([here, here], axis=0), jnp.concatenate([step, step], axis=0)], axis=1
        )
        t = jnp.dot(ss[...], z, preferred_element_type=F32)
        for c in range(2):
            tc = t[:, c * 128 : (c + 1) * 128].reshape(5, NX, NY, 128)
            x0 = jnp.where(i0 == 0, tc[:, 0], tc[:, 1])
            x1 = jnp.where(i0 == 0, tc[:, 1], tc[:, 2])
            pp[r, 2 * c] = x0
            pp[r, 2 * c + 1] = x1 - x0

    loop(ROWS, corners)

    def image(r, f0, f1, f2):
        donor = kq[r : r + 1, :]
        j0 = jnp.bitwise_and(jnp.right_shift(donor, 7), 15)
        at = iota((NY, 128), 0) - j0
        wy = jnp.where(at == 0, 1.0 - f1, jnp.where(at == 1, f1, 0.0))
        value = pp[r, 0] + f0 * pp[r, 1] + f2 * (pp[r, 2] + f0 * pp[r, 3])
        return jnp.sum(value * wy, axis=1)

    def row_of(ref, off, c):
        return ref[off * 8 + c : off * 8 + c + 1, :]

    sources = from_source(frac_copies)
    image_copies = {}
    for t in (1, 2, 3, 4, 5, 6, 7, 0):
        both = (OTHER[t], t)
        for off in both:
            if off:
                sources[off].wait_recv()
        for off in both:
            isend[off * 8 : off * 8 + 5, :] = image(off, *(row_of(frecv, off, c) for c in range(3)))
        fracs = unshare(*([row_of(frecv, off, 3 + c) for c in range(2)] for off in (t, OTHER[t])))
        value = image(16 + t, *fracs)
        low, high = share([value[v : v + 1] for v in range(5)])
        for c in range(3):
            isend[t * 8 + 5 + c : t * 8 + 6 + c, :] = low[c]
            isend[OTHER[t] * 8 + 5 + c : OTHER[t] * 8 + 6 + c, :] = high[c]
        for off in both:
            if off:
                image_copies[off] = message(isend, irecv.at[0], off, is_sem, ir_sem)
    irecv[0, 0:8] = isend[0:8]
    by_source = from_source(image_copies)
    raw_copies = beside(stv.at[0], [stv.at[1], stv.at[2]], 1)

    loads[4].wait()
    nt = (((1,), (1,)), ((), ()))

    def places(b):
        for row in range(ROWS):
            where = slice(PLACE[row] * 128, PLACE[row] * 128 + 128)
            cell = cq[b, row : row + 1, :]
            j = jnp.right_shift(cell, 7)
            column = jnp.bitwise_or(jnp.bitwise_and(jnp.right_shift(cell, 3), 128), jnp.bitwise_and(cell, 127))
            line = jnp.bitwise_or(jnp.left_shift(jnp.right_shift(cell, 11), 3), jnp.bitwise_and(j, 7))
            bs[b, :, where] = jnp.where(iota((256, 128), 0) == column, 1.0, 0.0).astype(BF16)
            i48 = iota((48, 128), 0)
            want = jnp.bitwise_or(jnp.left_shift(jnp.right_shift(i48, 4), 3), jnp.bitwise_and(i48, 7))
            ohs[b, :, where] = jnp.where(want == line, 1.0, 0.0).astype(BF16)
        count = lax.dot_general(ohs[b], bs[b], nt, preferred_element_type=F32).reshape(NX, 2, 8, 256)
        maskv[b, :, 0:8] = count[:, 0, :, 0:128]
        maskv[b, :, 8:16] = count[:, 0, :, 128:256]

    def spread(b, rows):
        for row in rows:
            where = slice(PLACE[row] * 128, PLACE[row] * 128 + 128)
            if row < 16:
                ghost = [irecv[b, row * 8 + v : row * 8 + v + 1, :] for v in range(5)]
            else:
                ends = (row - 16, OTHER[row - 16])
                low, high = ([irecv[b, a * 8 + 5 + c : a * 8 + 6 + c, :] for c in range(3)] for a in ends)
                ghost = unshare(low, high)
            lines = ohs[b, :, where].reshape(NX, 16, 128)
            for v in range(5):
                g = jnp.broadcast_to(SIGN[v] * ghost[v], (8, 128))
                hi = g.astype(BF16)
                lo = (g - hi.astype(F32)).astype(BF16)
                both = jnp.concatenate([hi, lo], axis=0)
                am[b, v * 48 : (v + 1) * 48, where] = (lines * both[None]).reshape(48, 128)

    def collect(b, rows):
        where = slice(PLACE[rows[0]] * 128, (PLACE[rows[-1]] + 1) * 128)
        return lax.dot_general(am[b, :, where], bs[b, :, where], nt, preferred_element_type=F32)

    def filled(b, total, tile):
        total = total.reshape(5, NX, 2, 8, 256)[..., tile * 128 : (tile + 1) * 128]
        rows = slice(tile * 8, tile * 8 + 8)
        return jnp.where(maskv[b, :, rows][None] > 0.5, total[:, :, 0] + total[:, :, 1], stv[b, :, :, rows])

    places(0)
    arrived(list_copies)
    places(1)
    places(2)
    onward = []

    def pass_on(i):
        rows = slice(PARTS[i].start * 8, PARTS[i].stop * 8)
        for off in range(PARTS[i].start, PARTS[i].stop):
            if off:
                by_source[off].wait_recv()
        onward.append(beside(irecv.at[0, rows], [irecv.at[1, rows], irecv.at[2, rows]], 2 + i))

    pass_on(0)
    pass_on(1)
    spread(0, NEAR)
    near = collect(0, NEAR)
    pass_on(2)
    spread(0, FAR)
    total = near + collect(0, FAR)
    for tile in range(2):
        fil[:, :, tile * 8 : tile * 8 + 8] = filled(0, total, tile)
    halos = {
        name: (
            pltpu.make_async_remote_copy(
                src_ref=src, dst_ref=dst, send_sem=hs_sem.at[i], recv_sem=hr_sem.at[i], device_id=where, device_id_type=MESH
            ),
            sends,
            receives,
        )
        for i, (name, src, dst, where, sends, receives) in enumerate(
            (
                ("yl", fil.at[:, :, 13:16, :], yl.at[:, :, 5:8, :], {"gy": above}, has_above, has_below),
                ("yr", fil.at[:, :, 0:3, :], yr.at[:, :, 0:3, :], {"gy": below}, has_below, has_above),
            )
        )
    }
    for copy, sends, _ in halos.values():
        pl.when(sends)(copy.start)

    u = [fil[v] for v in range(5)]
    rinv, p = inverse_pressure(u)
    for v, pair in enumerate(split(u, rinv, p, 2, lf[2])):
        for s in range(2):
            fz[s, v * NX : (v + 1) * NX] = pair[s]
    for v, pair in enumerate(split(u, rinv, p, 1, lf[1])):
        for s in range(2):
            for i in range(NX):
                fy[pl.ds((s * 32 + 8) * 16 + v * NX + i, 16, 16), :] = pair[s][i]
    for v, pair in enumerate(split(u, rinv, p, 0, lf[0])):
        for s in range(2):
            fx[s, v, 3:6] = pair[s]

    def along_z(n):
        chg[n] = z_change(fz[0, n], fz[1, n])

    loop(15, along_z)

    for side in (1, 2):
        arrived([onward[0][side - 1], onward[1][side - 1]])
        spread(side, NEAR)
        part[side - 1] = collect(side, NEAR)
    arrived(halos.values())
    for edge, ref, row, base in ((~has_below, yl, 0, 0), (~has_above, yr, 15, 24)):
        u = [jnp.where(edge, fil[v, :, row : row + 1, :], ref[v]) for v in range(5)]
        rinv, p = inverse_pressure(u)
        for v, pair in enumerate(split(u, rinv, p, 1, lf[1])):
            for s in range(2):
                for i in range(NX):
                    fy[pl.ds((s * 32 + base) * 16 + v * NX + i, 8, 16), :] = pair[s][i]

    def along_y(n):
        b, h = n // 2, n % 2

        def window(s, start, count):
            return jnp.stack([fy[pl.ds(pl.multiple_of((s * 32 + start + q) * 16 + h * 8, 8), 8), :] for q in range(count)])

        flux = upwind(*betas(window(0, 5 + 3 * b, 7))) + downwind(*betas(window(1, 6 + 3 * b, 7)))
        for q in range(3):
            fluxy[pl.ds(pl.multiple_of((3 * b + q) * 16 + h * 8, 8), 8), :] = flux[q]

    loop(12, along_y)
    for n in range(15):
        chg[n] = chg[n] + (fluxy[pl.ds(16 + n, 16, 16), :] - fluxy[pl.ds(n, 16, 16), :])

    arrived(raw_copies)
    for side, edge, row, base in ((1, ~has_left, 0, 0), (2, ~has_right, 2, 6)):
        arrived([onward[2][side - 1]])
        spread(side, FAR)
        total = part[side - 1] + collect(side, FAR)
        for tile in range(2):
            rows = slice(tile * 8, tile * 8 + 8)
            brick = filled(side, total, tile)
            u = [jnp.where(edge, fil[v, row : row + 1, rows], brick[v]) for v in range(5)]
            rinv, p = inverse_pressure(u)
            for v, pair in enumerate(split(u, rinv, p, 0, lf[0])):
                for s in range(2):
                    fx[s, v, base : base + 3, rows] = pair[s]
    def along_x(n):
        v, h = n // 2, n % 2
        rows = pl.ds(pl.multiple_of(h * 8, 8), 8)
        flux = upwind(*betas(fx[0, v, 0:8, rows])) + downwind(*betas(fx[1, v, 1:9, rows]))
        change = flux[1:] - flux[:-1] + chg[pl.ds(v * NX, NX), rows]
        mine = fil[v, :, rows]
        out[v, :, rows] = jnp.where(maskv[0, :, rows] > 0.5, mine, mine - (0.125 / 6.0) * change)

    loop(10, along_x)
    for copy in [*frac_copies.values(), *image_copies.values()]:
        copy.wait_send()
    for copy, sends, _ in [*halos.values(), *list_copies, *raw_copies, *onward[0], *onward[1], *onward[2]]:
        pl.when(sends)(copy.wait_send)


def solution(mesh):
    n_gx, n_gy = mesh.shape["gx"], mesh.shape["gy"]

    def on_device(state, lf_speed, ghost_cell, ghost_frac, donor_block):
        hbm = pl.BlockSpec(memory_space=pltpu.HBM)
        vmem = pltpu.VMEM
        dma = pltpu.SemaphoreType.DMA
        brick = (5, NX, NY, NZ)
        return pl.pallas_call(
            functools.partial(kernel, n_gx, n_gy),
            out_shape=jax.ShapeDtypeStruct(brick, F32),
            in_specs=[hbm] * 5,
            out_specs=pl.BlockSpec(memory_space=pltpu.VMEM),
            scratch_shapes=[
                vmem((3,) + brick, F32),
                vmem((16, 192), jnp.int32),
                vmem((3, 16, 192), F32),
                vmem((16, 192), jnp.int32),
                vmem((128, 128), F32),
                vmem((128, 128), F32),
                vmem((128, 128), F32),
                vmem((3, 128, 128), F32),
                vmem((ROWS, 128), jnp.int32),
                vmem((3, ROWS, 128), jnp.int32),
                vmem((240, 256), BF16),
                vmem((ROWS, 4, 5, NY, 128), F32),
                vmem((3, 256, ROWS * 128), BF16),
                vmem((3, 48, ROWS * 128), BF16),
                vmem((3, 240, ROWS * 128), BF16),
                vmem((3, NX, NY, NZ), F32),
                vmem((2, 240, 256), F32),
                vmem(brick, F32),
                vmem((5, NX, 8, NZ), F32),
                vmem((5, NX, 8, NZ), F32),
                vmem((2, 5, 9, NY, NZ), F32),
                vmem((2 * 32 * 16, NZ), F32),
                vmem((2, 15, NY, NZ), F32),
                vmem((18 * 16, NZ), F32),
                vmem((15, NY, NZ), F32),
                pltpu.SMEM((3,), F32),
                dma((5,)),
                dma((n_gy - 1,)),
                dma((n_gy - 1,)),
                dma((n_gy - 1,)),
                dma((n_gy - 1,)),
                dma((2,)),
                dma((2,)),
                dma((10,)),
                dma((10,)),
            ],
            compiler_params=pltpu.CompilerParams(
                collective_id=0, has_side_effects=True, vmem_limit_bytes=40 * 1024 * 1024
            ),
        )(
            *(
                pltpu.with_memory_space_constraint(x, pltpu.HBM)
                for x in (
                    lf_speed,
                    state,
                    ghost_cell.reshape(ghost_cell.shape[2:]),
                    ghost_frac.reshape((3,) + ghost_frac.shape[3:]),
                    donor_block.reshape(donor_block.shape[2:]),
                )
            )
        )

    return jax.shard_map(
        on_device,
        mesh=mesh,
        in_specs=(
            P(None, "gx", "gy", None),
            P(),
            P("gx", "gy", None, None),
            P(None, "gx", "gy", None, None),
            P("gx", "gy", None, None),
        ),
        out_specs=P(None, "gx", "gy", None),
        check_vma=False,
    )
```

time: 41.3 us -> 37.7 us (0.913)
  Pallas kernels: 39.3 us -> 36.3 us
  local copies, waits for them, and re-layouts: 1.56 us -> 0.65 us
    pallas_call x1, Pallas kernels: 39.3 us -> 36.3 us  [on_device(): pl.pallas_call(functools.partial(kernel, n_gx, n_gy), out_shape=jax.Shape...]
    unnamed x1, local copies, waits for them, and re-layouts: 1.56 us -> 0.65 us
where the time goes in v3:
time: 37.7 us; the launch traced here: 37 us
  Pallas kernels  36.3 us (96%)
  local copies, waits for them, and re-layouts  0.65 us (2%)
    pallas_call x1, Pallas kernels, on_device(): pl.pallas_call(functools.partial(kernel, n_gx, n_gy), out_shape=jax.Shape...  36.3 us

profile of v3, /device:TPU:15, one launch (start us, length us, event | category | flops | bytes accessed | tf_op | source)
XLA Modules:
  0.0 37.0 jit_solution(9309149263917272321)
XLA Ops:
  0.0 36.3 %shard_map.55 = f32[5,3,16,128]{3,2,1,0:T(8,128)S(1)} custom-call(f32[3]{0:T(128)} %lf_h.1, f32[5,3,16,128]{3,2,1,0:T(8,128)} %state_h.1, s32[16,192]{1,0:T(8,128)} %bitcast.4, f32[3,16,192]{2,1,0:T(8,128)} %bitcast.3, s32[16,192]{1,0:T(8,128)} %bitcast.5), custom_call_target="tpu_custom_call" | custom-call | tf_op jit(solution)/shard_map/pallas_call | solution.py:460
  36.3 0.7 %copy.7 = f32[5,3,16,128]{3,2,1,0:T(8,128)} copy(f32[5,3,16,128]{3,2,1,0:T(8,128)S(1)} %shard_map.55) | data formatting | bytes 245760

commit v4 on v3

--- a/solution.py
+++ b/solution.py
@@ -112,23 +112,24 @@
 
 
 OTHER = [8, 15, 14, 13, 12, 11, 10, 9]
-NEAR = [0, 1, 2, 3, 4, 5, 11, 12, 13, 14, 15, 16 + 1, 16 + 2, 16 + 3, 16 + 4, 16 + 5]
-FAR = [6, 7, 8, 9, 10, 16 + 6, 16 + 7, 16 + 0]
+NEAR = [0, 1, 2, 3, 4, 5, 6, 10, 11, 12, 13, 14, 15, 16 + 1, 16 + 2, 16 + 3, 16 + 4, 16 + 5, 16 + 6]
+FAR = [7, 8, 9, 16 + 7, 16 + 0]
 ORDER = NEAR + FAR
 PLACE = {row: place for place, row in enumerate(ORDER)}
-PARTS = (slice(0, 6), slice(11, 16), slice(6, 11))
+PARTS = (slice(0, 7), slice(10, 16), slice(7, 10))
 
 
 def kernel(
     n_gx, n_gy, lf_h, state_h, cell_h, frac_h, donor_h, out,
-    stv, cellv, fracv, donv, fsend, frecv, isend, irecv, kq, cq, ss, pp, bs, ohs, am, maskv, part,
+    stv, cellv, fracv, donv, fsend, frecv, isend, irecv, kq, cq, ss, pp, bs, ohs, am, maskv,
     fil, yl, yr, fx, fy, fz, fluxy, chg, lf,
-    in_sem, fs_sem, fr_sem, is_sem, ir_sem, hs_sem, hr_sem, xs_sem, xr_sem,
+    in_sem, fs_sem, fr_sem, is_sem, ir_sem, hs_sem, hr_sem, xs_sem, xr_sem, here_sem,
 ):
     gx, gy = lax.axis_index("gx"), lax.axis_index("gy")
     right, left, above, below = gx + 1, gx - 1, gy + 1, gy - 1
     has_left, has_right, has_below, has_above = gx > 0, gx < n_gx - 1, gy > 0, gy < n_gy - 1
     half = iota((1, 128), 1) < 64
+    even = lax.rem(gx, 2) == 0
 
     loads = [
         pltpu.make_async_copy(src, dst, in_sem.at[i])
@@ -147,7 +148,7 @@
         pl.semaphore_signal(barrier, inc=1, device_id={"gy": partner(off)}, device_id_type=MESH)
     for inside, other in ((has_left, left), (has_right, right)):
 
-        @pl.when(inside)
+        @pl.when(inside & even)
         def _():
             pl.semaphore_signal(barrier, inc=1, device_id={"gx": other}, device_id_type=MESH)
 
@@ -183,7 +184,8 @@
         fsend[pl.ds(3 + c, 8, 8), :] = low[c]
         for t, off in enumerate(OTHER):
             fsend[off * 8 + 3 + c : off * 8 + 4 + c, :] = high[c][t : t + 1]
-    pl.semaphore_wait(barrier, n_gy - 1 + has_left.astype(jnp.int32) + has_right.astype(jnp.int32))
+    beside_me = has_left.astype(jnp.int32) + has_right.astype(jnp.int32)
+    pl.semaphore_wait(barrier, n_gy - 1 + jnp.where(even, 0, beside_me))
 
     def message(send, recv, off, s_sem, r_sem):
         copy = pltpu.make_async_remote_copy(
@@ -205,9 +207,8 @@
     frecv[0:8] = fsend[0:8]
 
     def beside(src, dsts, i):
-        result = []
-        for side, (other, sends, receives) in enumerate(((right, has_right, has_left), (left, has_left, has_right))):
-            copy = pltpu.make_async_remote_copy(
+        return [
+            pltpu.make_async_remote_copy(
                 src_ref=src,
                 dst_ref=dsts[side],
                 send_sem=xs_sem.at[2 * i + side],
@@ -215,21 +216,20 @@
                 device_id={"gx": other},
                 device_id_type=MESH,
             )
-            pl.when(sends)(copy.start)
-            result.append((copy, sends, receives))
-        return result
-
-    def arrived(copies):
-        for copy, _, receives in copies:
-            pl.when(receives)(copy.wait_recv)
+            for side, other in enumerate((right, left))
+        ]
+
+    for inside, other, side in ((has_left, left, 1), (has_right, right, 0)):
+
+        @pl.when(inside & ~even)
+        def _():
+            pl.semaphore_signal(here_sem.at[side], inc=1, device_id={"gx": other}, device_id_type=MESH)
 
     loads[3].wait()
     loads[2].wait()
     main, tail = by_distance(cellv)
     packed = jnp.concatenate([main, tail], axis=0)
     cq[0] = jnp.where(packed < 0, -4096, packed)
-    list_copies = beside(cq.at[0], [cq.at[1], cq.at[2]], 0)
-
     loads[1].wait()
     main, tail = by_distance(donv)
     kq[...] = jnp.concatenate([main, tail], axis=0)
@@ -290,7 +290,6 @@
                 image_copies[off] = message(isend, irecv.at[0], off, is_sem, ir_sem)
     irecv[0, 0:8] = isend[0:8]
     by_source = from_source(image_copies)
-    raw_copies = beside(stv.at[0], [stv.at[1], stv.at[2]], 1)
 
     loads[4].wait()
     nt = (((1,), (1,)), ((), ()))
@@ -336,26 +335,39 @@
         rows = slice(tile * 8, tile * 8 + 8)
         return jnp.where(maskv[b, :, rows][None] > 0.5, total[:, :, 0] + total[:, :, 1], stv[b, :, :, rows])
 
+    list_copies = beside(cq.at[0], [cq.at[1], cq.at[2]], 0)
+    raw_copies = beside(stv.at[0], [stv.at[1], stv.at[2]], 1)
+    slices = [slice(part.start * 8, part.stop * 8) for part in PARTS]
+    passed = [beside(irecv.at[0, rows], [irecv.at[1, rows], irecv.at[2, rows]], 2 + i) for i, rows in enumerate(slices)]
+    side_copies = [list_copies, raw_copies] + passed
+
+    near_left = has_left & (lax.rem(gx, 8) != 0)
+    far_left = has_left & (lax.rem(gx, 8) == 0)
+
+    def start(copies):
+        pl.when(has_right)(copies[0].start)
+        pl.when(near_left)(copies[1].start)
+
+    def arrived(copies, side):
+        pl.when((has_left, has_right)[side])(copies[side].wait_recv)
+
+    def answered(side, expected):
+        @pl.when(expected & even)
+        def _():
+            pl.semaphore_wait(here_sem.at[side], 1)
+
+    answered(0, near_left)
+    answered(1, has_right)
+    start(list_copies)
+    start(raw_copies)
     places(0)
-    arrived(list_copies)
-    places(1)
-    places(2)
-    onward = []
-
-    def pass_on(i):
-        rows = slice(PARTS[i].start * 8, PARTS[i].stop * 8)
-        for off in range(PARTS[i].start, PARTS[i].stop):
+    for i, part in enumerate(PARTS):
+        for off in range(part.start, part.stop):
             if off:
                 by_source[off].wait_recv()
-        onward.append(beside(irecv.at[0, rows], [irecv.at[1, rows], irecv.at[2, rows]], 2 + i))
-
-    pass_on(0)
-    pass_on(1)
-    spread(0, NEAR)
-    near = collect(0, NEAR)
-    pass_on(2)
-    spread(0, FAR)
-    total = near + collect(0, FAR)
+        start(passed[i])
+    spread(0, ORDER)
+    total = collect(0, ORDER)
     for tile in range(2):
         fil[:, :, tile * 8 : tile * 8 + 8] = filled(0, total, tile)
     halos = {
@@ -394,11 +406,8 @@
 
     loop(15, along_z)
 
-    for side in (1, 2):
-        arrived([onward[0][side - 1], onward[1][side - 1]])
-        spread(side, NEAR)
-        part[side - 1] = collect(side, NEAR)
-    arrived(halos.values())
+    for copy, _, receives in halos.values():
+        pl.when(receives)(copy.wait_recv)
     for edge, ref, row, base in ((~has_below, yl, 0, 0), (~has_above, yr, 15, 24)):
         u = [jnp.where(edge, fil[v, :, row : row + 1, :], ref[v]) for v in range(5)]
         rinv, p = inverse_pressure(u)
@@ -421,11 +430,19 @@
     for n in range(15):
         chg[n] = chg[n] + (fluxy[pl.ds(16 + n, 16, 16), :] - fluxy[pl.ds(n, 16, 16), :])
 
-    arrived(raw_copies)
-    for side, edge, row, base in ((1, ~has_left, 0, 0), (2, ~has_right, 2, 6)):
-        arrived([onward[2][side - 1]])
+    answered(0, far_left)
+    for copies in side_copies:
+        pl.when(far_left)(copies[1].start)
+    for side, edge, row, base in ((2, ~has_right, 2, 6), (1, ~has_left, 0, 0)):
+        arrived(list_copies, side - 1)
+        places(side)
+        for copies in (raw_copies, passed[0], passed[1]):
+            arrived(copies, side - 1)
+        spread(side, NEAR)
+        total = collect(side, NEAR)
+        arrived(passed[2], side - 1)
         spread(side, FAR)
-        total = part[side - 1] + collect(side, FAR)
+        total = total + collect(side, FAR)
         for tile in range(2):
             rows = slice(tile * 8, tile * 8 + 8)
             brick = filled(side, total, tile)
@@ -445,8 +462,11 @@
     loop(10, along_x)
     for copy in [*frac_copies.values(), *image_copies.values()]:
         copy.wait_send()
-    for copy, sends, _ in [*halos.values(), *list_copies, *raw_copies, *onward[0], *onward[1], *onward[2]]:
+    for copy, sends, _ in halos.values():
         pl.when(sends)(copy.wait_send)
+    for copies in side_copies:
+        pl.when(has_right)(copies[0].wait_send)
+        pl.when(has_left)(copies[1].wait_send)
 
 
 def solution(mesh):
@@ -479,7 +499,6 @@
                 vmem((3, 48, ROWS * 128), BF16),
                 vmem((3, 240, ROWS * 128), BF16),
                 vmem((3, NX, NY, NZ), F32),
-                vmem((2, 240, 256), F32),
                 vmem(brick, F32),
                 vmem((5, NX, 8, NZ), F32),
                 vmem((5, NX, 8, NZ), F32),
@@ -498,6 +517,7 @@
                 dma((2,)),
                 dma((10,)),
                 dma((10,)),
+                pltpu.SemaphoreType.REGULAR((2,)),
             ],
             compiler_params=pltpu.CompilerParams(
                 collective_id=0, has_side_effects=True, vmem_limit_bytes=40 * 1024 * 1024

time: 37.7 us -> 37.8 us (level)
  the two profiles are of different devices: /device:TPU:15 before, /device:TPU:1 now
where the time goes in v4:
time: 37.8 us; the launch traced here: 37.6 us
  Pallas kernels  37 us (98%)
  local copies, waits for them, and re-layouts  0.65 us (2%)
    pallas_call x1, Pallas kernels, on_device(): pl.pallas_call(functools.partial(kernel, n_gx, n_gy), out_shape=jax.Shape...  37 us

profile of v4, /device:TPU:1, one launch (start us, length us, event | category | flops | bytes accessed | tf_op | source)
XLA Modules:
  0.0 37.6 jit_solution(15091261747197973042)
XLA Ops:
  0.0 37.0 %shard_map.55 = f32[5,3,16,128]{3,2,1,0:T(8,128)S(1)} custom-call(f32[3]{0:T(128)} %lf_h.1, f32[5,3,16,128]{3,2,1,0:T(8,128)} %state_h.1, s32[16,192]{1,0:T(8,128)} %bitcast.4, f32[3,16,192]{2,1,0:T(8,128)} %bitcast.3, s32[16,192]{1,0:T(8,128)} %bitcast.5), custom_call_target="tpu_custom_call" | custom-call | tf_op jit(solution)/shard_map/pallas_call | solution.py:480
  37.0 0.7 %copy.7 = f32[5,3,16,128]{3,2,1,0:T(8,128)} copy(f32[5,3,16,128]{3,2,1,0:T(8,128)S(1)} %shard_map.55) | data formatting | bytes 245760

commit v5 on v4

--- a/solution.py
+++ b/solution.py
@@ -122,14 +122,35 @@
 def kernel(
     n_gx, n_gy, lf_h, state_h, cell_h, frac_h, donor_h, out,
     stv, cellv, fracv, donv, fsend, frecv, isend, irecv, kq, cq, ss, pp, bs, ohs, am, maskv,
-    fil, yl, yr, fx, fy, fz, fluxy, chg, lf,
-    in_sem, fs_sem, fr_sem, is_sem, ir_sem, hs_sem, hr_sem, xs_sem, xr_sem, here_sem,
+    fil, beyond, yl, yr, fx, fy, fz, fluxy, chg, lf,
+    in_sem, fs_sem, fr_sem, is_sem, ir_sem, hs_sem, hr_sem, xs_sem, xr_sem, ds_sem, dr_sem, here_sem,
 ):
     gx, gy = lax.axis_index("gx"), lax.axis_index("gy")
     right, left, above, below = gx + 1, gx - 1, gy + 1, gy - 1
     has_left, has_right, has_below, has_above = gx > 0, gx < n_gx - 1, gy > 0, gy < n_gy - 1
     half = iota((1, 128), 1) < 64
     even = lax.rem(gx, 2) == 0
+    near_left = has_left & (lax.rem(gx, 8) != 0)
+    far_left = has_left & (lax.rem(gx, 8) == 0)
+    far_right = has_right & (lax.rem(gx, 8) == 7)
+
+    def partner(off):
+        return lax.rem(gy + off, n_gy)
+
+    barrier = pltpu.get_barrier_semaphore()
+    for off in sorted(range(1, n_gy), key=lambda off: -min(off, n_gy - off)):
+        pl.semaphore_signal(barrier, inc=1, device_id={"gy": partner(off)}, device_id_type=MESH)
+    for inside, other in ((near_left, left), (has_right, right)):
+
+        @pl.when(inside & even)
+        def _():
+            pl.semaphore_signal(barrier, inc=1, device_id={"gx": other}, device_id_type=MESH)
+
+    @pl.when(far_left)
+    def _():
+        for off in range(n_gy):
+            where = {"gx": left, "gy": partner(off)}
+            pl.semaphore_signal(barrier, inc=1, device_id=where, device_id_type=MESH)
 
     loads = [
         pltpu.make_async_copy(src, dst, in_sem.at[i])
@@ -139,18 +160,6 @@
     ]
     for load in loads:
         load.start()
-
-    def partner(off):
-        return lax.rem(gy + off, n_gy)
-
-    barrier = pltpu.get_barrier_semaphore()
-    for off in sorted(range(1, n_gy), key=lambda off: -min(off, n_gy - off)):
-        pl.semaphore_signal(barrier, inc=1, device_id={"gy": partner(off)}, device_id_type=MESH)
-    for inside, other in ((has_left, left), (has_right, right)):
-
-        @pl.when(inside & even)
-        def _():
-            pl.semaphore_signal(barrier, inc=1, device_id={"gx": other}, device_id_type=MESH)
 
     def turn(x):
         return pltpu.roll(x, 64, x.ndim - 1)
@@ -184,7 +193,7 @@
         fsend[pl.ds(3 + c, 8, 8), :] = low[c]
         for t, off in enumerate(OTHER):
             fsend[off * 8 + 3 + c : off * 8 + 4 + c, :] = high[c][t : t + 1]
-    beside_me = has_left.astype(jnp.int32) + has_right.astype(jnp.int32)
+    beside_me = has_left.astype(jnp.int32) + jnp.where(far_right, n_gy, has_right.astype(jnp.int32))
     pl.semaphore_wait(barrier, n_gy - 1 + jnp.where(even, 0, beside_me))
 
     def message(send, recv, off, s_sem, r_sem):
@@ -272,6 +281,18 @@
 
     sources = from_source(frac_copies)
     image_copies = {}
+    direct = {
+        off: pltpu.make_async_remote_copy(
+            src_ref=isend.at[pl.ds(off * 8, 8), :],
+            dst_ref=irecv.at[1, pl.ds((n_gy - off) % n_gy * 8, 8), :],
+            send_sem=ds_sem.at[off],
+            recv_sem=dr_sem.at[(n_gy - off) % n_gy],
+            device_id={"gx": right, "gy": partner(off)},
+            device_id_type=MESH,
+        )
+        for off in range(n_gy)
+    }
+    from_left = {(n_gy - off) % n_gy: copy for off, copy in direct.items()}
     for t in (1, 2, 3, 4, 5, 6, 7, 0):
         both = (OTHER[t], t)
         for off in both:
@@ -285,6 +306,8 @@
         for c in range(3):
             isend[t * 8 + 5 + c : t * 8 + 6 + c, :] = low[c]
             isend[OTHER[t] * 8 + 5 + c : OTHER[t] * 8 + 6 + c, :] = high[c]
+        for off in both:
+            pl.when(far_right)(direct[off].start)
         for off in both:
             if off:
                 image_copies[off] = message(isend, irecv.at[0], off, is_sem, ir_sem)
@@ -341,11 +364,8 @@
     passed = [beside(irecv.at[0, rows], [irecv.at[1, rows], irecv.at[2, rows]], 2 + i) for i, rows in enumerate(slices)]
     side_copies = [list_copies, raw_copies] + passed
 
-    near_left = has_left & (lax.rem(gx, 8) != 0)
-    far_left = has_left & (lax.rem(gx, 8) == 0)
-
-    def start(copies):
-        pl.when(has_right)(copies[0].start)
+    def start(copies, to_right=has_right):
+        pl.when(to_right)(copies[0].start)
         pl.when(near_left)(copies[1].start)
 
     def arrived(copies, side):
@@ -361,11 +381,19 @@
     start(list_copies)
     start(raw_copies)
     places(0)
+    arrived(list_copies, 1)
+    places(2)
+
+    @pl.when(near_left)
+    def _():
+        list_copies[0].wait_recv()
+        places(1)
+
     for i, part in enumerate(PARTS):
         for off in range(part.start, part.stop):
             if off:
                 by_source[off].wait_recv()
-        start(passed[i])
+        start(passed[i], has_right & ~far_right)
     spread(0, ORDER)
     total = collect(0, ORDER)
     for tile in range(2):
@@ -433,24 +461,48 @@
     answered(0, far_left)
     for copies in side_copies:
         pl.when(far_left)(copies[1].start)
-    for side, edge, row, base in ((2, ~has_right, 2, 6), (1, ~has_left, 0, 0)):
-        arrived(list_copies, side - 1)
-        places(side)
-        for copies in (raw_copies, passed[0], passed[1]):
-            arrived(copies, side - 1)
-        spread(side, NEAR)
-        total = collect(side, NEAR)
-        arrived(passed[2], side - 1)
-        spread(side, FAR)
-        total = total + collect(side, FAR)
-        for tile in range(2):
-            rows = slice(tile * 8, tile * 8 + 8)
-            brick = filled(side, total, tile)
-            u = [jnp.where(edge, fil[v, row : row + 1, rows], brick[v]) for v in range(5)]
-            rinv, p = inverse_pressure(u)
-            for v, pair in enumerate(split(u, rinv, p, 0, lf[0])):
-                for s in range(2):
-                    fx[s, v, base : base + 3, rows] = pair[s]
+    @pl.when(far_left)
+    def _():
+        list_copies[0].wait_recv()
+        places(1)
+
+    def parts_arrived(side, which):
+        for i in which:
+            if side == 2:
+                arrived(passed[i], 1)
+            else:
+                pl.when(near_left)(passed[i][0].wait_recv)
+
+                @pl.when(far_left)
+                def _():
+                    for off in range(PARTS[i].start, PARTS[i].stop):
+                        from_left[off].wait_recv()
+
+    for side, inside, row, base in ((2, has_right, 2, 6), (1, has_left, 0, 0)):
+
+        @pl.when(inside)
+        def _():
+            parts_arrived(side, (0, 1))
+            spread(side, NEAR)
+            total = collect(side, NEAR)
+            parts_arrived(side, (2,))
+            spread(side, FAR)
+            total = total + collect(side, FAR)
+            arrived(raw_copies, side - 1)
+            for tile in range(2):
+                beyond[:, :, tile * 8 : tile * 8 + 8] = filled(side, total, tile)
+
+        @pl.when(~inside)
+        def _():
+            for i in range(NX):
+                beyond[:, i] = fil[:, row]
+
+        u = [beyond[v] for v in range(5)]
+        rinv, p = inverse_pressure(u)
+        for v, pair in enumerate(split(u, rinv, p, 0, lf[0])):
+            for s in range(2):
+                fx[s, v, base : base + 3] = pair[s]
+
     def along_x(n):
         v, h = n // 2, n % 2
         rows = pl.ds(pl.multiple_of(h * 8, 8), 8)
@@ -465,8 +517,11 @@
     for copy, sends, _ in halos.values():
         pl.when(sends)(copy.wait_send)
     for copies in side_copies:
-        pl.when(has_right)(copies[0].wait_send)
+        to_right = has_right if copies is list_copies or copies is raw_copies else has_right & ~far_right
+        pl.when(to_right)(copies[0].wait_send)
         pl.when(has_left)(copies[1].wait_send)
+    for copy in direct.values():
+        pl.when(far_right)(copy.wait_send)
 
 
 def solution(mesh):
@@ -500,6 +555,7 @@
                 vmem((3, 240, ROWS * 128), BF16),
                 vmem((3, NX, NY, NZ), F32),
                 vmem(brick, F32),
+                vmem(brick, F32),
                 vmem((5, NX, 8, NZ), F32),
                 vmem((5, NX, 8, NZ), F32),
                 vmem((2, 5, 9, NY, NZ), F32),
@@ -517,6 +573,8 @@
                 dma((2,)),
                 dma((10,)),
                 dma((10,)),
+                dma((n_gy,)),
+                dma((n_gy,)),
                 pltpu.SemaphoreType.REGULAR((2,)),
             ],
             compiler_params=pltpu.CompilerParams(

time: 37.8 us -> 35.8 us (0.947)
  the two profiles are of different devices: /device:TPU:1 before, /device:TPU:15 now
where the time goes in v5:
time: 35.8 us; the launch traced here: 35.3 us
  Pallas kernels  34.7 us (97%)
  local copies, waits for them, and re-layouts  0.65 us (2%)
    pallas_call x1, Pallas kernels, on_device(): pl.pallas_call(functools.partial(kernel, n_gx, n_gy), out_shape=jax.Shape...  34.7 us

profile of v5, /device:TPU:15, one launch (start us, length us, event | category | flops | bytes accessed | tf_op | source)
XLA Modules:
  0.0 35.3 jit_solution(14915634627863226976)
XLA Ops:
  0.0 34.7 %shard_map.55 = f32[5,3,16,128]{3,2,1,0:T(8,128)S(1)} custom-call(f32[3]{0:T(128)} %lf_h.1, f32[5,3,16,128]{3,2,1,0:T(8,128)} %state_h.1, s32[16,192]{1,0:T(8,128)} %bitcast.4, f32[3,16,192]{2,1,0:T(8,128)} %bitcast.3, s32[16,192]{1,0:T(8,128)} %bitcast.5), custom_call_target="tpu_custom_call" | custom-call | tf_op jit(solution)/shard_map/pallas_call | solution.py:535
  34.7 0.7 %copy.7 = f32[5,3,16,128]{3,2,1,0:T(8,128)} copy(f32[5,3,16,128]{3,2,1,0:T(8,128)S(1)} %shard_map.55) | data formatting | bytes 245760

commit v6 on v5

--- a/solution.py
+++ b/solution.py
@@ -122,7 +122,7 @@
 def kernel(
     n_gx, n_gy, lf_h, state_h, cell_h, frac_h, donor_h, out,
     stv, cellv, fracv, donv, fsend, frecv, isend, irecv, kq, cq, ss, pp, bs, ohs, am, maskv,
-    fil, beyond, yl, yr, fx, fy, fz, fluxy, chg, lf,
+    fil, beyond, yl, yr, fx, fy, fz, fluxy, chg, ahead, lf,
     in_sem, fs_sem, fr_sem, is_sem, ir_sem, hs_sem, hr_sem, xs_sem, xr_sem, ds_sem, dr_sem, here_sem,
 ):
     gx, gy = lax.axis_index("gx"), lax.axis_index("gy")
@@ -205,7 +205,6 @@
             device_id={"gy": partner(off)},
             device_id_type=MESH,
         )
-        copy.start()
         return copy
 
     def from_source(copies):
@@ -213,6 +212,8 @@
 
     offs = [off for t in (0, 7, 6, 5, 4, 3, 2, 1) for off in (OTHER[t], t) if off]
     frac_copies = {off: message(fsend, frecv, off, fs_sem, fr_sem) for off in offs}
+    for copy in frac_copies.values():
+        copy.start()
     frecv[0:8] = fsend[0:8]
 
     def beside(src, dsts, i):
@@ -267,6 +268,11 @@
             pp[r, 2 * c + 1] = x1 - x0
 
     loop(ROWS, corners)
+
+    list_copies = beside(cq.at[0], [cq.at[1], cq.at[2]], 0)
+    raw_copies = beside(stv.at[0], [stv.at[1], stv.at[2]], 1)
+    for copies in (list_copies, raw_copies):
+        pl.when(far_right)(copies[0].start)
 
     def image(r, f0, f1, f2):
         donor = kq[r : r + 1, :]
@@ -311,6 +317,9 @@
         for off in both:
             if off:
                 image_copies[off] = message(isend, irecv.at[0], off, is_sem, ir_sem)
+                pl.when(~far_right)(image_copies[off].start)
+    for off in offs:
+        pl.when(far_right)(image_copies[off].start)
     irecv[0, 0:8] = isend[0:8]
     by_source = from_source(image_copies)
 
@@ -358,8 +367,6 @@
         rows = slice(tile * 8, tile * 8 + 8)
         return jnp.where(maskv[b, :, rows][None] > 0.5, total[:, :, 0] + total[:, :, 1], stv[b, :, :, rows])
 
-    list_copies = beside(cq.at[0], [cq.at[1], cq.at[2]], 0)
-    raw_copies = beside(stv.at[0], [stv.at[1], stv.at[2]], 1)
     slices = [slice(part.start * 8, part.stop * 8) for part in PARTS]
     passed = [beside(irecv.at[0, rows], [irecv.at[1, rows], irecv.at[2, rows]], 2 + i) for i, rows in enumerate(slices)]
     side_copies = [list_copies, raw_copies] + passed
@@ -378,8 +385,8 @@
 
     answered(0, near_left)
     answered(1, has_right)
-    start(list_copies)
-    start(raw_copies)
+    start(list_copies, has_right & ~far_right)
+    start(raw_copies, has_right & ~far_right)
     places(0)
     arrived(list_copies, 1)
     places(2)
@@ -478,6 +485,12 @@
                     for off in range(PARTS[i].start, PARTS[i].stop):
                         from_left[off].wait_recv()
 
+    def ahead_x(n):
+        v, h = n // 2, n % 2
+        rows = pl.ds(pl.multiple_of(h * 8, 8), 8)
+        ahead[0:1, v, rows] = upwind(*betas(fx[0, v, 3:8, rows]))
+        ahead[1:3, v, rows] = downwind(*betas(fx[1, v, 3:9, rows]))
+
     for side, inside, row, base in ((2, has_right, 2, 6), (1, has_left, 0, 0)):
 
         @pl.when(inside)
@@ -502,11 +515,15 @@
         for v, pair in enumerate(split(u, rinv, p, 0, lf[0])):
             for s in range(2):
                 fx[s, v, base : base + 3] = pair[s]
+        if side == 2:
+            loop(10, ahead_x)
 
     def along_x(n):
         v, h = n // 2, n % 2
         rows = pl.ds(pl.multiple_of(h * 8, 8), 8)
-        flux = upwind(*betas(fx[0, v, 0:8, rows])) + downwind(*betas(fx[1, v, 1:9, rows]))
+        up, down = upwind(*betas(fx[0, v, 0:7, rows])), downwind(*betas(fx[1, v, 1:7, rows]))
+        flux = [up[0] + down[0], up[1] + down[1], up[2] + ahead[1, v, rows], ahead[0, v, rows] + ahead[2, v, rows]]
+        flux = jnp.stack(flux)
         change = flux[1:] - flux[:-1] + chg[pl.ds(v * NX, NX), rows]
         mine = fil[v, :, rows]
         out[v, :, rows] = jnp.where(maskv[0, :, rows] > 0.5, mine, mine - (0.125 / 6.0) * change)
@@ -563,6 +580,7 @@
                 vmem((2, 15, NY, NZ), F32),
                 vmem((18 * 16, NZ), F32),
                 vmem((15, NY, NZ), F32),
+                vmem((3, 5, NY, NZ), F32),
                 pltpu.SMEM((3,), F32),
                 dma((5,)),
                 dma((n_gy - 1,)),

time: 35.8 us -> 35.2 us (0.983)
  Pallas kernels: 34.7 us -> 34.1 us
    pallas_call x1, Pallas kernels: 34.7 us -> 34.1 us  [on_device(): pl.pallas_call(functools.partial(kernel, n_gx, n_gy), out_shape=jax.Shape...]
where the time goes in v6:
time: 35.2 us; the launch traced here: 34.8 us
  Pallas kernels  34.1 us (97%)
  local copies, waits for them, and re-layouts  0.65 us (2%)
    pallas_call x1, Pallas kernels, on_device(): pl.pallas_call(functools.partial(kernel, n_gx, n_gy), out_shape=jax.Shape...  34.1 us

profile of v6, /device:TPU:15, one launch (start us, length us, event | category | flops | bytes accessed | tf_op | source)
XLA Modules:
  0.0 34.8 jit_solution(17611498235389626565)
XLA Ops:
  0.0 34.1 %shard_map.55 = f32[5,3,16,128]{3,2,1,0:T(8,128)S(1)} custom-call(f32[3]{0:T(128)} %lf_h.1, f32[5,3,16,128]{3,2,1,0:T(8,128)} %state_h.1, s32[16,192]{1,0:T(8,128)} %bitcast.4, f32[3,16,192]{2,1,0:T(8,128)} %bitcast.3, s32[16,192]{1,0:T(8,128)} %bitcast.5), custom_call_target="tpu_custom_call" | custom-call | tf_op jit(solution)/shard_map/pallas_call | solution.py:552
  34.1 0.7 %copy.7 = f32[5,3,16,128]{3,2,1,0:T(8,128)} copy(f32[5,3,16,128]{3,2,1,0:T(8,128)S(1)} %shard_map.55) | data formatting | bytes 245760

commit v7 on v6

--- a/solution.py
+++ b/solution.py
@@ -485,6 +485,18 @@
                     for off in range(PARTS[i].start, PARTS[i].stop):
                         from_left[off].wait_recv()
 
+    def sent():
+        for copy in [*frac_copies.values(), *image_copies.values()]:
+            copy.wait_send()
+        for copy, sends, _ in halos.values():
+            pl.when(sends)(copy.wait_send)
+        for copies in side_copies:
+            to_right = has_right if copies is list_copies or copies is raw_copies else has_right & ~far_right
+            pl.when(to_right)(copies[0].wait_send)
+            pl.when(has_left)(copies[1].wait_send)
+        for copy in direct.values():
+            pl.when(far_right)(copy.wait_send)
+
     def ahead_x(n):
         v, h = n // 2, n % 2
         rows = pl.ds(pl.multiple_of(h * 8, 8), 8)
@@ -517,6 +529,7 @@
                 fx[s, v, base : base + 3] = pair[s]
         if side == 2:
             loop(10, ahead_x)
+            sent()
 
     def along_x(n):
         v, h = n // 2, n % 2
@@ -529,16 +542,6 @@
         out[v, :, rows] = jnp.where(maskv[0, :, rows] > 0.5, mine, mine - (0.125 / 6.0) * change)
 
     loop(10, along_x)
-    for copy in [*frac_copies.values(), *image_copies.values()]:
-        copy.wait_send()
-    for copy, sends, _ in halos.values():
-        pl.when(sends)(copy.wait_send)
-    for copies in side_copies:
-        to_right = has_right if copies is list_copies or copies is raw_copies else has_right & ~far_right
-        pl.when(to_right)(copies[0].wait_send)
-        pl.when(has_left)(copies[1].wait_send)
-    for copy in direct.values():
-        pl.when(far_right)(copy.wait_send)
 
 
 def solution(mesh):

time: 35.2 us -> 35.1 us (level)
  no operation moved by 1% of the time
where the time goes in v7:
time: 35.1 us; the launch traced here: 34.7 us
  Pallas kernels  34 us (97%)
  local copies, waits for them, and re-layouts  0.65 us (2%)
    pallas_call x1, Pallas kernels, on_device(): pl.pallas_call(functools.partial(kernel, n_gx, n_gy), out_shape=jax.Shape...  34 us

profile of v7, /device:TPU:15, one launch (start us, length us, event | category | flops | bytes accessed | tf_op | source)
XLA Modules:
  0.0 34.7 jit_solution(17718829356622014146)
XLA Ops:
  0.0 34.0 %shard_map.55 = f32[5,3,16,128]{3,2,1,0:T(8,128)S(1)} custom-call(f32[3]{0:T(128)} %lf_h.1, f32[5,3,16,128]{3,2,1,0:T(8,128)} %state_h.1, s32[16,192]{1,0:T(8,128)} %bitcast.4, f32[3,16,192]{2,1,0:T(8,128)} %bitcast.3, s32[16,192]{1,0:T(8,128)} %bitcast.5), custom_call_target="tpu_custom_call" | custom-call | tf_op jit(solution)/shard_map/pallas_call | solution.py:555
  34.0 0.7 %copy.7 = f32[5,3,16,128]{3,2,1,0:T(8,128)} copy(f32[5,3,16,128]{3,2,1,0:T(8,128)S(1)} %shard_map.55) | data formatting | bytes 245760
